TPU v7x, 32 devices: a whole 2x2x4 slice. The times are simulated.
32 devices in a mesh: dom: 2 (over core), gx: 4 (over y, x), gy: 4 (over z).
Axes of the slice: x: 2, y: 2, z: 4, core: 2. Of those that a mesh axis runs over, the one named last changes fastest.
Arguments:
- wind: float32 [2, 3, 64, 64, 128], P('dom', None, 'gx', 'gy'), may hold values from -6 to 6
- adjoint: float32 [2, 4, 64, 64, 128], P('dom', None, 'gx', 'gy'), may hold values from -6 to 6
- turbines: int32 [64, 64, 128], P('gx', 'gy'), may hold values 0 or 1
- fringe_range: int32 [2], replicated, may hold values from 8 to 63, as said below
Outputs:
- earlier: float32 [2, 4, 64, 64, 128], P('dom', None, 'gx', 'gy')
Inputs may be any that keep to these rules, and one draw needn't show every extreme that they name: `fringe_range`: element 0 is the first streamwise cell of the fringe, the last cell 64 - 1 of the domain, and element 1 its length in cells, from 8 to 16; the fringe wraps around the periodic streamwise dimension.
All inputs are finite; a program needn't handle non-finite values. No bound on the sum of `turbines` on one device may be relied on, other than what follows from the above.
Results may differ from a plain program's by a relative error of at most 0.00002.
Values sent between devices are 32-bit elements; how exact they have to be, the bound alone decides.
A program may use at most 64 MiB of HBM per device.

v0:
```python
import math

import jax
import jax.numpy as jnp
from jax import lax
from jax.sharding import PartitionSpec as P

DT = 0.1
SMAG = 0.1
SOUND_SQ = 4.0
DRAG = 1.0
RATE = 3.0


def padded_2(shard, sides, width):
    for axis, dim in sides:
        devices, length = (lax.axis_size(axis), shard.shape[dim])
        up = [(i, (i + 1) % devices) for i in range(devices)]
        down = [(j, i) for i, j in up]
        last = lax.slice_in_dim(shard, length - width, length, axis=dim)
        leading = lax.slice_in_dim(shard, 0, width, axis=dim)
        before = lax.ppermute(last, axis, up)
        after = lax.ppermute(leading, axis, down)
        shard = jnp.concatenate([before, shard, after], axis=dim)
    return shard


def passed_along(shard, axis, by):
    devices = lax.axis_size(axis)
    pairs = [(i, i + by) for i in range(devices) if 0 <= i + by < devices]
    return lax.ppermute(shard, axis, pairs)


def crop_xy(field, margin):
    if margin == 0:
        return field
    return field[..., margin : field.shape[-3] - margin, margin : field.shape[-2] - margin, :]


def pad_z(field):
    return jnp.pad(field, [(0, 0)] * (field.ndim - 1) + [(1, 1)])


def diff_x(field):
    return 0.5 * (field[..., 2:, 1:-1, :] - field[..., :-2, 1:-1, :])


def diff_y(field):
    return 0.5 * (field[..., 1:-1, 2:, :] - field[..., 1:-1, :-2, :])


def diff_z(field):
    padded = crop_xy(pad_z(field), 1)
    return 0.5 * (padded[..., 2:] - padded[..., :-2])


def eddy(wind_ext):
    grads = (diff_x(wind_ext), diff_y(wind_ext), diff_z(wind_ext))
    strain_sq = jnp.zeros_like(grads[0][0])
    for first in range(3):
        for second in range(3):
            strain = 0.5 * (grads[first][second] + grads[second][first])
            strain_sq = strain_sq + strain * strain
    return SMAG * jnp.sqrt(2.0 * strain_sq)


def spread(field, viscosity):
    centre = crop_xy(field, 1)
    visc_mid = crop_xy(viscosity, 1)
    flux_xp = (viscosity[..., 2:, 1:-1, :] + visc_mid) * 0.5 * (field[..., 2:, 1:-1, :] - centre)
    flux_xm = (visc_mid + viscosity[..., :-2, 1:-1, :]) * 0.5 * (centre - field[..., :-2, 1:-1, :])
    flux_yp = (viscosity[..., 1:-1, 2:, :] + visc_mid) * 0.5 * (field[..., 1:-1, 2:, :] - centre)
    flux_ym = (visc_mid + viscosity[..., 1:-1, :-2, :]) * 0.5 * (centre - field[..., 1:-1, :-2, :])
    visc_pad = pad_z(visc_mid)
    field_pad = pad_z(centre)
    flux_zp = (visc_pad[..., 2:] + visc_mid) * 0.5 * (field_pad[..., 2:] - centre)
    flux_zm = (visc_mid + visc_pad[..., :-2]) * 0.5 * (centre - field_pad[..., :-2])
    return flux_xp - flux_xm + flux_yp - flux_ym + flux_zp - flux_zm


def tendency(adjoint_ext, wind_here, viscosity, drag_cells):
    along_x = diff_x(adjoint_ext)
    along_y = diff_y(adjoint_ext)
    along_z = diff_z(adjoint_ext)
    advection = wind_here[0] * along_x + wind_here[1] * along_y + wind_here[2] * along_z
    diffusion = spread(adjoint_ext[:3], viscosity)
    wind_speed = jnp.sqrt(
        wind_here[0] * wind_here[0] + wind_here[1] * wind_here[1] + wind_here[2] * wind_here[2]
    )
    centre = crop_xy(adjoint_ext, 1)
    acoustic = SOUND_SQ * jnp.stack([along_x[3], along_y[3], along_z[3]], 0)
    velocity = advection[:3] + diffusion + acoustic - DRAG * drag_cells * wind_speed * centre[:3]
    pressure = advection[3] + along_x[0] + along_y[1] + along_z[2]
    return (centre, jnp.concatenate([velocity, pressure[None]], 0))


def ramp(position, fringe_range, length_total):
    offset = jnp.mod(position - fringe_range[0], length_total)
    fringe_width = fringe_range[1]
    fringe_phase = math.pi * (offset.astype(jnp.float32) + 0.5) / fringe_width.astype(jnp.float32)
    sine = jnp.sin(fringe_phase)
    return jnp.where(offset < fringe_width, RATE * sine * sine, 0.0)


def on_device(wind, adjoint, turbines, fringe_range):
    is_main = lax.axis_index("dom") == 0
    cells_x = wind.shape[2]
    length_total = cells_x * lax.axis_size("gx")
    anchor = lax.axis_index("gx") * cells_x
    background = jnp.concatenate([wind[0], turbines[None].astype(jnp.float32)], 0)
    reach = 3
    first_width = 2
    extended = padded_2(background, (("gx", 1), ("gy", 2)), reach)
    first_ext = padded_2(adjoint[0], (("gx", 1), ("gy", 2)), first_width)
    viscosity = eddy(extended[:3])
    drag_cells = jnp.where(is_main, extended[3], 0.0)

    def advance(adjoint_ext, extent):
        margin = reach - (extent - 1)
        wind_here = crop_xy(extended[:3], margin)
        drag_here = crop_xy(drag_cells, margin)
        visc_here = crop_xy(viscosity, reach - 1 - extent)
        position = anchor + jnp.arange(-(extent - 1), cells_x + extent - 1, dtype=jnp.int32)
        fringe_rates = ramp(position, fringe_range, length_total)[:, None, None]
        centre, rate_term = tendency(adjoint_ext, wind_here, visc_here, drag_here)
        forcing = fringe_rates * centre[:3]
        incoming = passed_along(forcing, "dom", 1)
        own_part = jnp.where(is_main, forcing, 0.0)
        velocity = centre[:3] + DT * (rate_term[:3] - own_part + incoming)
        pressure = centre[3:] + DT * rate_term[3:]
        return jnp.concatenate([velocity, pressure], 0)

    current = advance(first_ext, first_width)
    current = advance(current, 1)
    return current[None]


def solution(mesh):
    in_specs = (
        P("dom", None, "gx", "gy", None),
        P("dom", None, "gx", "gy", None),
        P("gx", "gy", None),
        P(),
    )
    out_specs = P("dom", None, "gx", "gy", None)
    return jax.shard_map(
        on_device, mesh=mesh, in_specs=in_specs, out_specs=out_specs, check_vma=False
    )
```

profile of v0, /device:TPU:0, one launch (start us, length us, event | category | flops | bytes accessed | tf_op | source)
XLA Modules:
  0.0 37.8 jit_solution(15086202103934329516)
XLA Ops:
  0.0 1.0 %convert_bitcast_fusion = f32[1,16,16,128]{3,2,1,0:T(8,128)S(1)} fusion(s32[16,16,128]{2,1,0:T(8,128)} %param.6), kind=kLoop, calls=%fused_computation.187 | loop fusion | flops 32768 | bytes 262144 | tf_op jit(solution)/shard_map/convert_element_type | solution.py:110
  1.0 0.9 %pad_maximum_fusion.9 = (f32[4,3,16,128]{3,2,1,0:T(8,128)S(1)}, f32[4,3,16,128]{3,2,1,0:T(8,128)S(1)}) fusion(f32[1,16,16,128]{3,2,1,0:T(8,128)S(1)} %convert_bitcast_fusion, f32[3,16,16,128]{3,2,1,0:T(8,128)} %bitcast.70), kind=kLoop, calls=%fused_computation.189 | loop fusion | flops 49152 | bytes 720896 | tf_op jit(solution)/shard_map/slice | solution.py:20
  2.0 3.0 %collective-permute-start.4 = (f32[4,3,16,128]{3,2,1,0:T(8,128)S(1)}, f32[4,3,16,128]{3,2,1,0:T(8,128)S(1)}, u32[]{:S(2)}, u32[]{:S(2)}) collective-permute-start(f32[4,3,16,128]{3,2,1,0:T(8,128)S(1)} %get-tuple-element.36), channel_id=1, source_target_pairs={{0,4},{4,8},{8,12},{12,0},{1,5},{5,9},{9,13},{13,1},{2,6},{6,10},{... | collective-permute-start | bytes 294920 | tf_op jit(solution)/shard_map/ppermute | solution.py:22
  5.0 1.0 %collective-permute-start.5 = (f32[4,3,16,128]{3,2,1,0:T(8,128)S(1)}, f32[4,3,16,128]{3,2,1,0:T(8,128)S(1)}, u32[]{:S(2)}, u32[]{:S(2)}) collective-permute-start(f32[4,3,16,128]{3,2,1,0:T(8,128)S(1)} %get-tuple-element.37), channel_id=1, source_target_pairs={{4,0},{8,4},{12,8},{0,12},{5,1},{9,5},{13,9},{1,13},{6,2},{10,6},{... | collective-permute-start | bytes 294920 | tf_op jit(solution)/shard_map/ppermute | solution.py:23
  6.0 0.9 %fusion.108 = (f32[4,2,16,128]{3,2,1,0:T(8,128)S(1)}, f32[4,2,16,128]{3,2,1,0:T(8,128)S(1)}) fusion(f32[4,16,16,128]{3,2,1,0:T(8,128)} %bitcast.73), kind=kLoop, calls=%fused_computation.207 | loop fusion | bytes 262144 | tf_op jit(solution)/shard_map/slice | solution.py:20
  6.9 1.1 %collective-permute-start = (f32[4,2,16,128]{3,2,1,0:T(8,128)S(1)}, f32[4,2,16,128]{3,2,1,0:T(8,128)S(1)}, u32[]{:S(2)}, u32[]{:S(2)}) collective-permute-start(f32[4,2,16,128]{3,2,1,0:T(8,128)S(1)} %get-tuple-element.38), channel_id=1, source_target_pairs={{0,4},{4,8},{8,12},{12,0},{1,5},{5,9},{9,13},{13,1},{2,6},{6,10},{... | collective-permute-start | bytes 196616 | tf_op jit(solution)/shard_map/ppermute | solution.py:22
  7.9 1.9 %collective-permute-start.1 = (f32[4,2,16,128]{3,2,1,0:T(8,128)S(1)}, f32[4,2,16,128]{3,2,1,0:T(8,128)S(1)}, u32[]{:S(2)}, u32[]{:S(2)}) collective-permute-start(f32[4,2,16,128]{3,2,1,0:T(8,128)S(1)} %get-tuple-element.39), channel_id=1, source_target_pairs={{4,0},{8,4},{12,8},{0,12},{5,1},{9,5},{13,9},{1,13},{6,2},{10,6},{... | collective-permute-start | bytes 196616 | tf_op jit(solution)/shard_map/ppermute | solution.py:23
  9.9 0.7 %fusion.109 = (s32[1]{0:T(128)}, s32[1]{0:T(128)}) fusion(s32[2]{0:T(128)S(1)} %copy-done.2), kind=kLoop, calls=%fused_computation.208 | loop fusion | bytes 16 | tf_op jit(solution)/shard_map/slice | solution.py:98
  11.3 1.4 %compare_select_fusion.5 = f32[18]{0:T(128)S(1)} fusion(f32[]{:T(128)S(6)} %convert_element_type.41, s32[]{:T(128)} %bitcast.15, s32[]{:T(128)} %bitcast.14, s32[]{:T(128)S(6)} %mul.532), kind=kLoop, calls=%fused_computation.199 | loop fusion | flops 396 | bytes 88 | tf_op jit(solution)/shard_map/jit(_where)/select_n | solution.py:102
  12.7 1.4 %compare_select_fusion.4 = f32[16]{0:T(128)S(1)} fusion(f32[]{:T(128)S(6)} %convert_element_type.41, s32[]{:T(128)} %bitcast.15, s32[]{:T(128)} %bitcast.14, s32[]{:T(128)S(6)} %mul.532), kind=kLoop, calls=%fused_computation.197 | loop fusion | flops 336 | bytes 80 | tf_op jit(solution)/shard_map/jit(_where)/select_n | solution.py:102
  14.1 2.0 %collective-permute-start.2 = (f32[4,20,2,128]{3,2,1,0:T(2,128)S(1)}, f32[4,20,2,128]{3,2,1,0:T(2,128)S(1)}, u32[]{:S(2)}, u32[]{:S(2)}) collective-permute-start(f32[4,20,2,128]{3,2,1,0:T(2,128)S(1)} %get-tuple-element.30), channel_id=1, source_target_pairs={{0,1},{1,2},{2,3},{3,0},{4,5},{5,6},{6,7},{7,4},{8,9},{9,10},{10,1... | collective-permute-start | bytes 245768 | tf_op jit(solution)/shard_map/ppermute | solution.py:22
  16.2 2.1 %collective-permute-start.3 = (f32[4,20,2,128]{3,2,1,0:T(2,128)S(1)}, f32[4,20,2,128]{3,2,1,0:T(2,128)S(1)}, u32[]{:S(2)}, u32[]{:S(2)}) collective-permute-start(f32[4,20,2,128]{3,2,1,0:T(2,128)S(1)} %get-tuple-element.31), channel_id=1, source_target_pairs={{1,0},{2,1},{3,2},{0,3},{5,4},{6,5},{7,6},{4,7},{9,8},{10,9},{11,1... | collective-permute-start | bytes 245768 | tf_op jit(solution)/shard_map/ppermute | solution.py:23
  18.4 3.8 %collective-permute-start.7 = (f32[4,22,3,128]{3,2,1,0:T(4,128)S(1)}, f32[4,22,3,128]{3,2,1,0:T(4,128)S(1)}, u32[]{:S(2)}, u32[]{:S(2)}) collective-permute-start(f32[4,22,3,128]{3,2,1,0:T(4,128)S(1)} %get-tuple-element.25), channel_id=1, source_target_pairs={{1,0},{2,1},{3,2},{0,3},{5,4},{6,5},{7,6},{4,7},{9,8},{10,9},{11,1... | collective-permute-start | bytes 405512 | tf_op jit(solution)/shard_map/ppermute | solution.py:23
  22.2 2.5 %collective-permute-done.3 = f32[4,20,2,128]{3,2,1,0:T(2,128)S(1)} collective-permute-done((f32[4,20,2,128]{3,2,1,0:T(2,128)S(1)}, f32[4,20,2,128]{3,2,1,0:T(2,128)S(1)}, u32[]{:S(2)}, u32[]{:S(2)}) %collective-permute-start.3) | collective-permute-done | bytes 81952 | tf_op jit(solution)/shard_map/ppermute | solution.py:23
  25.1 1.3 %collective-permute-start.8 = (f32[3,18,18,128]{3,2,1,0:T(8,128)S(1)}, f32[3,18,18,128]{3,2,1,0:T(8,128)S(1)}, u32[]{:S(2)}, u32[]{:S(2)}) collective-permute-start(f32[3,18,18,128]{3,2,1,0:T(8,128)S(1)} %get-tuple-element.15), channel_id=1, source_target_pairs={{0,16},{1,17},{2,18},{3,19},{4,20},{5,21},{6,22},{7,23},{8,24},{9,... | collective-permute-start | bytes 1493000 | tf_op jit(solution)/shard_map/ppermute | solution.py:31
  26.6 1.1 %collective-permute-done.6 = f32[4,22,3,128]{3,2,1,0:T(4,128)S(1)} collective-permute-done((f32[4,22,3,128]{3,2,1,0:T(4,128)S(1)}, f32[4,22,3,128]{3,2,1,0:T(4,128)S(1)}, u32[]{:S(2)}, u32[]{:S(2)}) %collective-permute-start.6) | collective-permute-done | bytes 135200 | tf_op jit(solution)/shard_map/ppermute | solution.py:22
  27.7 1.3 %collective-permute-done.7 = f32[4,22,3,128]{3,2,1,0:T(4,128)S(1)} collective-permute-done((f32[4,22,3,128]{3,2,1,0:T(4,128)S(1)}, f32[4,22,3,128]{3,2,1,0:T(4,128)S(1)}, u32[]{:S(2)}, u32[]{:S(2)}) %collective-permute-start.7) | collective-permute-done | bytes 135200 | tf_op jit(solution)/shard_map/ppermute | solution.py:23
  29.3 0.6 %fusion.4 = (f32[3,20,20,128]{3,2,1,0:T(8,128)S(1)}, f32[3,20,20,128]{3,2,1,0:T(8,128)S(1)}, f32[3,20,20,128]{3,2,1,0:T(8,128)S(1)}) fusion(f32[4,22,22,128]{3,2,1,0:T(8,128)S(1)} %pad_maximum_fusion.1, f32[3,22,22,128]{3,2,1,0:T(8,128)S(1)} %slice.480), kind=kLoop, calls=%fused_computation.32 | loop fusion | flops 921600 | bytes 5044224 | tf_op jit(solution)/shard_map/mul | solution.py:45
  30.8 1.0 %multiply_add_fusion = (f32[4,18,18,128]{3,2,1,0:T(8,128)S(1)}, f32[4,18,18,128]{3,2,1,0:T(8,128)S(1)}, f32[4,18,18,128]{3,2,1,0:T(8,128)S(1)}, f32[4,18,18,128]{3,2,1,0:T(8,128)S(1)}) fusion(f32[18,18,128]{2,1,0:T(8,128)S(1)} %get-tuple-element.13, f32[18,18,128]{2,1,0:T(8,128)S(1)} %get-tuple-element.14, f32[18,18,128]{2,1,0:T(8,128)S(1)} %get-tuple-element.12, ...), kind=kLoop, calls=%fused_computation.26 | loop fusion | flops 1990656 | bytes 7839744 | tf_op jit(solution)/shard_map/add | solution.py:85
  32.1 0.8 %fusion.15 = f32[3,18,18,128]{3,2,1,0:T(8,128)S(1)} fusion(f32[3,18,18,128]{3,2,1,0:T(8,128)S(1)} %get-tuple-element.16, f32[3,18,18,128]{3,2,1,0:T(8,128)S(1)} %collective-permute-done.8, f32[4,20,18,128]{3,2,1,0:T(8,128)S(1)} %get-tuple-element.29, f32[4,20,18,128]{3,2,1,0:T(8,128)S(1)} %get-tuple-element.28, f32[4,20,20,128]{3,2,1,0:T(8,128)S(1)} %pad_maximum_fusion.2, ...), kind=kLoop, calls=%fused_computation.43 | loop fusion | flops 3732480 | bytes 5640265 | tf_op jit(solution)/shard_map/add | solution.py:129
  33.0 0.6 %multiply_add_fusion.1 = (f32[4,16,16,128]{3,2,1,0:T(8,128)S(1)}, f32[4,16,16,128]{3,2,1,0:T(8,128)S(1)}, f32[4,16,16,128]{3,2,1,0:T(8,128)S(1)}, f32[4,16,16,128]{3,2,1,0:T(8,128)S(1)}) fusion(f32[16,16,128]{2,1,0:T(8,128)S(1)} %get-tuple-element.41, f32[16,16,128]{2,1,0:T(8,128)S(1)} %get-tuple-element.42, f32[16,16,128]{2,1,0:T(8,128)S(1)} %get-tuple-element.40, ...), kind=kLoop, calls=%fused_computation.68 | loop fusion | flops 1835008 | bytes 3817472 | tf_op jit(solution)/shard_map/add | solution.py:85
  33.8 1.3 %collective-permute-start.9 = (f32[3,16,16,128]{3,2,1,0:T(8,128)S(1)}, f32[3,16,16,128]{3,2,1,0:T(8,128)S(1)}, u32[]{:S(2)}, u32[]{:S(2)}) collective-permute-start(f32[3,16,16,128]{3,2,1,0:T(8,128)S(1)} %get-tuple-element.26), channel_id=1, source_target_pairs={{0,16},{1,17},{2,18},{3,19},{4,20},{5,21},{6,22},{7,23},{8,24},{9,... | collective-permute-start | bytes 1179656 | tf_op jit(solution)/shard_map/ppermute | solution.py:31
  35.3 1.2 %collective-permute-done.9 = f32[3,16,16,128]{3,2,1,0:T(8,128)S(1)} collective-permute-done((f32[3,16,16,128]{3,2,1,0:T(8,128)S(1)}, f32[3,16,16,128]{3,2,1,0:T(8,128)S(1)}, u32[]{:S(2)}, u32[]{:S(2)}) %collective-permute-start.9) | collective-permute-done | bytes 393248 | tf_op jit(solution)/shard_map/ppermute | solution.py:31
  37.0 0.8 %maximum_bitcast_fusion = f32[1,4,16,16,128]{4,3,2,1,0:T(8,128)} fusion(f32[1,16,16,128]{3,2,1,0:T(8,128)S(1)} %get-tuple-element.33, f32[3,16,16,128]{3,2,1,0:T(8,128)S(1)} %fusion.42), kind=kLoop, calls=%fused_computation.67 | loop fusion | flops 131072 | bytes 1048576 | tf_op jit(solution)/shard_map/broadcast_in_dim | solution.py:135
  (37 shorter events, 3.0 us)
Async XLA Ops:
  0.0 9.8 %copy-start = (f32[1,3,16,16,128]{4,3,2,1,0:T(8,128)S(1)}, f32[1,3,16,16,128]{4,3,2,1,0:T(8,128)}, u32[]{:S(2)}) copy-start(f32[1,3,16,16,128]{4,3,2,1,0:T(8,128)} %param.4) | copy-start | bytes 1179652
  0.0 14.1 %copy-start.1 = (f32[1,4,16,16,128]{4,3,2,1,0:T(8,128)S(1)}, f32[1,4,16,16,128]{4,3,2,1,0:T(8,128)}, u32[]{:S(2)}) copy-start(f32[1,4,16,16,128]{4,3,2,1,0:T(8,128)} %param.5) | copy-start | bytes 1572868
  0.0 9.9 %copy-start.2 = (s32[2]{0:T(128)S(1)}, s32[2]{0:T(128)}, u32[]{:S(2)}) copy-start(s32[2]{0:T(128)} %param.7) | copy-start | bytes 28
  2.0 16.3 %collective-permute-start.4 = (f32[4,3,16,128]{3,2,1,0:T(8,128)S(1)}, f32[4,3,16,128]{3,2,1,0:T(8,128)S(1)}, u32[]{:S(2)}, u32[]{:S(2)}) collective-permute-start(f32[4,3,16,128]{3,2,1,0:T(8,128)S(1)} %get-tuple-element.36), channel_id=1, source_target_pairs={{0,4},{4,8},{8,12},{12,0},{1,5},{5,9},{9,13},{13,1},{2,6},{6,10},{... | collective-permute-start | bytes 294920 | tf_op jit(solution)/shard_map/ppermute | solution.py:22
  5.0 13.3 %collective-permute-start.5 = (f32[4,3,16,128]{3,2,1,0:T(8,128)S(1)}, f32[4,3,16,128]{3,2,1,0:T(8,128)S(1)}, u32[]{:S(2)}, u32[]{:S(2)}) collective-permute-start(f32[4,3,16,128]{3,2,1,0:T(8,128)S(1)} %get-tuple-element.37), channel_id=1, source_target_pairs={{4,0},{8,4},{12,8},{0,12},{5,1},{9,5},{13,9},{1,13},{6,2},{10,6},{... | collective-permute-start | bytes 294920 | tf_op jit(solution)/shard_map/ppermute | solution.py:23
  6.9 7.2 %collective-permute-start = (f32[4,2,16,128]{3,2,1,0:T(8,128)S(1)}, f32[4,2,16,128]{3,2,1,0:T(8,128)S(1)}, u32[]{:S(2)}, u32[]{:S(2)}) collective-permute-start(f32[4,2,16,128]{3,2,1,0:T(8,128)S(1)} %get-tuple-element.38), channel_id=1, source_target_pairs={{0,4},{4,8},{8,12},{12,0},{1,5},{5,9},{9,13},{13,1},{2,6},{6,10},{... | collective-permute-start | bytes 196616 | tf_op jit(solution)/shard_map/ppermute | solution.py:22
  7.9 6.1 %collective-permute-start.1 = (f32[4,2,16,128]{3,2,1,0:T(8,128)S(1)}, f32[4,2,16,128]{3,2,1,0:T(8,128)S(1)}, u32[]{:S(2)}, u32[]{:S(2)}) collective-permute-start(f32[4,2,16,128]{3,2,1,0:T(8,128)S(1)} %get-tuple-element.39), channel_id=1, source_target_pairs={{4,0},{8,4},{12,8},{0,12},{5,1},{9,5},{13,9},{1,13},{6,2},{10,6},{... | collective-permute-start | bytes 196616 | tf_op jit(solution)/shard_map/ppermute | solution.py:23
  14.1 8.1 %collective-permute-start.2 = (f32[4,20,2,128]{3,2,1,0:T(2,128)S(1)}, f32[4,20,2,128]{3,2,1,0:T(2,128)S(1)}, u32[]{:S(2)}, u32[]{:S(2)}) collective-permute-start(f32[4,20,2,128]{3,2,1,0:T(2,128)S(1)} %get-tuple-element.30), channel_id=1, source_target_pairs={{0,1},{1,2},{2,3},{3,0},{4,5},{5,6},{6,7},{7,4},{8,9},{9,10},{10,1... | collective-permute-start | bytes 245768 | tf_op jit(solution)/shard_map/ppermute | solution.py:22
  16.2 8.6 %collective-permute-start.3 = (f32[4,20,2,128]{3,2,1,0:T(2,128)S(1)}, f32[4,20,2,128]{3,2,1,0:T(2,128)S(1)}, u32[]{:S(2)}, u32[]{:S(2)}) collective-permute-start(f32[4,20,2,128]{3,2,1,0:T(2,128)S(1)} %get-tuple-element.31), channel_id=1, source_target_pairs={{1,0},{2,1},{3,2},{0,3},{5,4},{6,5},{7,6},{4,7},{9,8},{10,9},{11,1... | collective-permute-start | bytes 245768 | tf_op jit(solution)/shard_map/ppermute | solution.py:23
  18.4 9.3 %collective-permute-start.6 = (f32[4,22,3,128]{3,2,1,0:T(4,128)S(1)}, f32[4,22,3,128]{3,2,1,0:T(4,128)S(1)}, u32[]{:S(2)}, u32[]{:S(2)}) collective-permute-start(f32[4,22,3,128]{3,2,1,0:T(4,128)S(1)} %get-tuple-element.24), channel_id=1, source_target_pairs={{0,1},{1,2},{2,3},{3,0},{4,5},{5,6},{6,7},{7,4},{8,9},{9,10},{10,1... | collective-permute-start | bytes 405512 | tf_op jit(solution)/shard_map/ppermute | solution.py:22
  18.4 10.6 %collective-permute-start.7 = (f32[4,22,3,128]{3,2,1,0:T(4,128)S(1)}, f32[4,22,3,128]{3,2,1,0:T(4,128)S(1)}, u32[]{:S(2)}, u32[]{:S(2)}) collective-permute-start(f32[4,22,3,128]{3,2,1,0:T(4,128)S(1)} %get-tuple-element.25), channel_id=1, source_target_pairs={{1,0},{2,1},{3,2},{0,3},{5,4},{6,5},{7,6},{4,7},{9,8},{10,9},{11,1... | collective-permute-start | bytes 405512 | tf_op jit(solution)/shard_map/ppermute | solution.py:23
  25.1 7.0 %collective-permute-start.8 = (f32[3,18,18,128]{3,2,1,0:T(8,128)S(1)}, f32[3,18,18,128]{3,2,1,0:T(8,128)S(1)}, u32[]{:S(2)}, u32[]{:S(2)}) collective-permute-start(f32[3,18,18,128]{3,2,1,0:T(8,128)S(1)} %get-tuple-element.15), channel_id=1, source_target_pairs={{0,16},{1,17},{2,18},{3,19},{4,20},{5,21},{6,22},{7,23},{8,24},{9,... | collective-permute-start | bytes 1493000 | tf_op jit(solution)/shard_map/ppermute | solution.py:31
  33.8 2.6 %collective-permute-start.9 = (f32[3,16,16,128]{3,2,1,0:T(8,128)S(1)}, f32[3,16,16,128]{3,2,1,0:T(8,128)S(1)}, u32[]{:S(2)}, u32[]{:S(2)}) collective-permute-start(f32[3,16,16,128]{3,2,1,0:T(8,128)S(1)} %get-tuple-element.26), channel_id=1, source_target_pairs={{0,16},{1,17},{2,18},{3,19},{4,20},{5,21},{6,22},{7,23},{8,24},{9,... | collective-permute-start | bytes 1179656 | tf_op jit(solution)/shard_map/ppermute | solution.py:31
where the time goes:
time: 38.1 us; the launch traced here: 37.8 us
  starting transfers between devices  17.6 us (46%)
  other arithmetic  11.5 us (30%)
  waiting for transfers between devices  6.12 us (16%)
  local copies, waits for them, and re-layouts  1.61 us (4%)
  between operations  0.94 us (2%)
    ppermute x4, starting transfers between devices, padded_2(): after = lax.ppermute(leading, axis, down)  8.84 us
    ppermute x4, starting transfers between devices, padded_2(): before = lax.ppermute(last, axis, up)  6.15 us
    ppermute x4, waiting for transfers between devices, padded_2(): after = lax.ppermute(leading, axis, down)  3.83 us
    select_n x2, other arithmetic, ramp(): return jnp.where(offset < fringe_width, RATE * sine * sine, 0.0)  2.79 us
    ppermute x2, starting transfers between devices, passed_along(): return lax.ppermute(shard, axis, pairs)  2.65 us
    add x2, other arithmetic, tendency(): wind_here[0] * along_x + wind_here[1] * along_y + wind_here[2] * along_z  1.63 us
    add x2, other arithmetic, advance(): velocity = centre[:3] + DT * (rate_term[:3] - own_part + incoming)  1.39 us
    ppermute x2, waiting for transfers between devices, passed_along(): return lax.ppermute(shard, axis, pairs)  1.17 us
  transfers between devices with their start and end apart: 10, of which 4 were waited for; matrix products, arithmetic and copies ran while one was open for 21% of the time, Pallas kernels for 0%

commit v1 on v0

v1 whole, which is shorter than its diff:
```python
import functools
import math

import jax
import jax.numpy as jnp
from jax import lax
from jax.experimental import pallas as pl
from jax.experimental.pallas import tpu as pltpu
from jax.sharding import PartitionSpec as P

DT = 0.1
SMAG = 0.1
SOUND_SQ = 4.0
DRAG = 1.0
RATE = 3.0
H = 0.5 * DT
GROUP = 2


def shifted_z(field):
    depth = field.shape[-1]
    lane = lax.broadcasted_iota(jnp.int32, field.shape, 1)
    after = jnp.where(lane == depth - 1, 0.0, pltpu.roll(field, depth - 1, 1))
    before = jnp.where(lane == 0, 0.0, pltpu.roll(field, 1, 1))
    return after, before


def shifted_y(field, row_after, row_before):
    rows = field.shape[0]
    row = lax.broadcasted_iota(jnp.int32, field.shape, 0)
    after = jnp.where(row == rows - 1, row_after, pltpu.roll(field, rows - 1, 0))
    before = jnp.where(row == 0, row_before, pltpu.roll(field, 1, 0))
    return after, before


def neighbours(ext, sides, c, x):
    here = ext[c, x + 1]
    yp, ym = shifted_y(here, sides[1, c, x], sides[0, c, x])
    zp, zm = shifted_z(here)
    return here, ext[c, x + 2], ext[c, x], yp, ym, zp, zm


def kernel(
    sizes,
    fringe,
    wind,
    wind_rows,
    adjoint,
    adjoint_rows,
    turbines,
    out,
    a_ext,
    w_ext,
    n_ext,
    b_ext,
    turb,
    coef,
    a_in,
    w_in,
    n_in,
    b_in,
    n_out,
    b_out,
    first_main,
    second_main,
    rates,
    load_sem,
    send_sem,
    recv_sem,
):
    n_gx, n_gy = sizes
    cells_x, cells_y, cells_z = turb.shape
    dom, gx, gy = (lax.axis_index(a) for a in ("dom", "gx", "gy"))
    total = cells_x * n_gx
    reach = total // 4 - 1
    is_main = dom == 0
    in_fringe = jnp.logical_or(gx == n_gx - 1, gx * cells_x < reach)
    sends_forcing = jnp.logical_and(is_main, in_fringe)
    gets_forcing = jnp.logical_and(jnp.logical_not(is_main), in_fringe)
    up_x, down_x = lax.rem(gx + 1, n_gx), lax.rem(gx + n_gx - 1, n_gx)
    up_y, down_y = lax.rem(gy + 1, n_gy), lax.rem(gy + n_gy - 1, n_gy)
    places = ({"gx": up_x}, {"gx": down_x}, {"gy": up_y}, {"gy": down_y})
    partner = {"dom": 1 - dom}

    def remote(src, dst, slot, device):
        return pltpu.make_async_remote_copy(
            src_ref=src,
            dst_ref=dst,
            send_sem=send_sem.at[slot],
            recv_sem=recv_sem.at[slot],
            device_id=device,
            device_id_type=pl.DeviceIdType.MESH,
        )

    load_wind = pltpu.make_async_copy(wind.at[0], w_ext.at[:, pl.ds(1, cells_x)], load_sem.at[0])
    load_adjoint = pltpu.make_async_copy(
        adjoint.at[0], a_ext.at[:, pl.ds(1, cells_x)], load_sem.at[1]
    )
    load_turbines = pltpu.make_async_copy(turbines, turb, load_sem.at[2])
    load_wind.start()

    barrier = pltpu.get_barrier_semaphore()
    for place in places + (partner,):
        pl.semaphore_signal(
            barrier, inc=1, device_id=place, device_id_type=pl.DeviceIdType.MESH
        )
    load_adjoint.start()
    load_turbines.start()

    position = gx * cells_x + lax.broadcasted_iota(jnp.int32, (cells_x, cells_z), 0)
    offset = position - fringe[0]
    offset = jnp.where(offset < 0, offset + total, offset)
    phase = math.pi * (offset.astype(jnp.float32) + 0.5) / fringe[1].astype(jnp.float32)
    sine = jnp.sin(phase)
    sign = jnp.where(is_main, -DT, DT)
    rates[...] = jnp.where(offset < fringe[1], sign * (RATE * sine * sine), 0.0)

    pl.semaphore_wait(barrier, len(places) + 1)

    def exchange(slot, ext, x_src, y_src, sides, lead):
        last, first = x_src
        pieces = (
            remote(last, ext.at[:, 0] if lead else ext.at[0], slot, places[0]),
            remote(
                first,
                ext.at[:, cells_x + 1] if lead else ext.at[cells_x + 1],
                slot + 1,
                places[1],
            ),
            remote(y_src[0], sides.at[0], slot + 2, places[2]),
            remote(y_src[1], sides.at[1], slot + 3, places[3]),
        )
        for k in (2, 3, 0, 1):
            pieces[k].start()
        return pieces

    wind_copies = exchange(
        0,
        w_ext,
        (wind.at[0, :, cells_x - 1], wind.at[0, :, 0]),
        (wind_rows.at[:, :, cells_y - 1], wind_rows.at[:, :, 0]),
        w_in,
        True,
    )
    adjoint_copies = exchange(
        4,
        a_ext,
        (adjoint.at[0, :, cells_x - 1], adjoint.at[0, :, 0]),
        (adjoint_rows.at[:, :, cells_y - 1], adjoint_rows.at[:, :, 0]),
        a_in,
        True,
    )
    first_forcing = remote(adjoint.at[0, pl.ds(0, 3)], first_main, 16, partner)

    @pl.when(sends_forcing)
    def _():
        first_forcing.start()

    load_wind.wait()
    for piece in wind_copies:
        piece.wait_recv()

    def viscosity(x):
        grads = []
        for c in range(3):
            _, xp, xm, yp, ym, zp, zm = neighbours(w_ext, w_in, c, x)
            grads.append((xp - xm, yp - ym, zp - zm))
        own = sum(grads[k][k] * grads[k][k] for k in range(3))
        xy = grads[0][1] + grads[1][0]
        xz = grads[0][2] + grads[2][0]
        yz = grads[1][2] + grads[2][1]
        nu = (0.5 * SMAG) * jnp.sqrt(2.0 * own + (xy * xy + xz * xz + yz * yz))
        n_ext[x + 1] = nu
        n_out[0, x] = nu[cells_y - 1 :]
        n_out[1, x] = nu[:1]

    def for_slabs(body):
        def step(i, carry):
            for k in range(GROUP):
                body(i * GROUP + k)
            return carry

        lax.fori_loop(0, cells_x // GROUP, step, 0)

    for_slabs(viscosity)
    viscosity_copies = exchange(
        8,
        n_ext,
        (n_ext.at[cells_x], n_ext.at[1]),
        (n_out.at[0], n_out.at[1]),
        n_in,
        False,
    )
    load_turbines.wait()
    load_adjoint.wait()
    for piece in adjoint_copies + viscosity_copies:
        piece.wait_recv()

    @pl.when(gets_forcing)
    def _():
        first_forcing.wait_recv()

    drag_scale = jnp.where(is_main, DT * DRAG, 0.0)

    def coefficients(x):
        nu, u, v, w = n_ext[x + 1], w_ext[0, x + 1], w_ext[1, x + 1], w_ext[2, x + 1]
        nxp, nxm = n_ext[x + 2] + nu, n_ext[x] + nu
        nyp, nym = shifted_y(nu, n_in[1, x], n_in[0, x])
        nzp, nzm = shifted_z(nu)
        nyp, nym, nzp, nzm = nyp + nu, nym + nu, nzp + nu, nzm + nu
        speed = jnp.sqrt(u * u + v * v + w * w)
        drag = drag_scale * turb[x].astype(jnp.float32) * speed
        around = (nxp + nxm) + (nyp + nym) + (nzp + nzm)
        return (
            1.0 - H * around - drag,
            H * (nxp + u),
            H * (nxm - u),
            H * (nyp + v),
            H * (nym - v),
            H * (nzp + w),
            H * (nzm - w),
        )

    def advance(ext, sides, main, weights, x):
        u, v, w = w_ext[0, x + 1], w_ext[1, x + 1], w_ext[2, x + 1]
        p, pxp, pxm, pyp, pym, pzp, pzm = neighbours(ext, sides, 3, x)
        slopes = (pxp - pxm, pyp - pym, pzp - pzm)
        gain = u * slopes[0] + v * slopes[1] + w * slopes[2]
        rate = rates[pl.ds(x, 1)]
        results = []
        for c in range(3):
            stencil = neighbours(ext, sides, c, x)
            gain = gain + (stencil[1 + 2 * c] - stencil[2 + 2 * c])
            new = sum(k * f for k, f in zip(weights, stencil))
            source = jnp.where(gets_forcing, main[c, x], stencil[0])
            results.append(new + (SOUND_SQ * H) * slopes[c] + rate * source)
        results.append(p + H * gain)
        return results

    def first_step(x):
        weights = coefficients(x)
        for k, weight in enumerate(weights):
            coef[k, x] = weight
        for c, new in enumerate(advance(a_ext, a_in, first_main, weights, x)):
            b_ext[c, x + 1] = new
            b_out[0, c, x] = new[cells_y - 1 :]
            b_out[1, c, x] = new[:1]

    for_slabs(first_step)
    second_copies = exchange(
        12,
        b_ext,
        (b_ext.at[:, cells_x], b_ext.at[:, 1]),
        (b_out.at[0], b_out.at[1]),
        b_in,
        True,
    )
    second_forcing = remote(
        b_ext.at[pl.ds(0, 3), pl.ds(1, cells_x)], second_main, 17, partner
    )

    @pl.when(sends_forcing)
    def _():
        second_forcing.start()

    for piece in second_copies:
        piece.wait_recv()

    @pl.when(gets_forcing)
    def _():
        second_forcing.wait_recv()

    def second_step(x):
        weights = tuple(coef[k, x] for k in range(7))
        for c, new in enumerate(advance(b_ext, b_in, second_main, weights, x)):
            out[0, c, x] = new

    for_slabs(second_step)

    for piece in wind_copies + adjoint_copies + viscosity_copies + second_copies:
        piece.wait_send()

    @pl.when(sends_forcing)
    def _():
        first_forcing.wait_send()
        second_forcing.wait_send()


def on_device(wind, adjoint, turbines, fringe_range):
    _, _, cx, cy, cz = wind.shape
    f32 = jnp.float32
    sizes = (lax.axis_size("gx"), lax.axis_size("gy"))
    anywhere = pl.BlockSpec(memory_space=pltpu.HBM)
    return pl.pallas_call(
        functools.partial(kernel, sizes),
        out_shape=jax.ShapeDtypeStruct(adjoint.shape, f32),
        in_specs=[pl.BlockSpec(memory_space=pltpu.SMEM)] + [anywhere] * 5,
        out_specs=pl.BlockSpec(memory_space=pltpu.VMEM),
        scratch_shapes=[
            pltpu.VMEM((4, cx + 2, cy, cz), f32),
            pltpu.VMEM((3, cx + 2, cy, cz), f32),
            pltpu.VMEM((cx + 2, cy, cz), f32),
            pltpu.VMEM((4, cx + 2, cy, cz), f32),
            pltpu.VMEM((cx, cy, cz), jnp.int32),
            pltpu.VMEM((7, cx, cy, cz), f32),
            pltpu.VMEM((2, 4, cx, 1, cz), f32),
            pltpu.VMEM((2, 3, cx, 1, cz), f32),
            pltpu.VMEM((2, cx, 1, cz), f32),
            pltpu.VMEM((2, 4, cx, 1, cz), f32),
            pltpu.VMEM((2, cx, 1, cz), f32),
            pltpu.VMEM((2, 4, cx, 1, cz), f32),
            pltpu.VMEM((3, cx, cy, cz), f32),
            pltpu.VMEM((3, cx, cy, cz), f32),
            pltpu.VMEM((cx, cz), f32),
            pltpu.SemaphoreType.DMA((3,)),
            pltpu.SemaphoreType.DMA((18,)),
            pltpu.SemaphoreType.DMA((18,)),
        ],
        compiler_params=pltpu.CompilerParams(
            collective_id=0, has_side_effects=True, vmem_limit_bytes=60 * 1024 * 1024
        ),
        name="adjoint_steps",
    )(
        fringe_range,
        wind,
        wind.reshape(3, cx, cy, 1, cz),
        adjoint,
        adjoint.reshape(4, cx, cy, 1, cz),
        turbines,
    )


def solution(mesh):
    in_specs = (
        P("dom", None, "gx", "gy", None),
        P("dom", None, "gx", "gy", None),
        P("gx", "gy", None),
        P(),
    )
    out_specs = P("dom", None, "gx", "gy", None)
    return jax.shard_map(
        on_device, mesh=mesh, in_specs=in_specs, out_specs=out_specs, check_vma=False
    )
```

time: 38.1 us -> 23.8 us (0.62)
  Pallas kernels: 0 us -> 21.7 us
  starting transfers between devices: 17.6 us -> 0 us
  other arithmetic: 11.5 us -> 0 us
  waiting for transfers between devices: 6.12 us -> 0 us
  between operations: 0.94 us -> 0.01 us
    pallas_call x0 -> x1, Pallas kernels: none -> 21.7 us  [on_device(): pl.pallas_call(functools.partial(kernel, sizes), out_shape=jax.ShapeDtype...]
    ppermute x10 -> x0, starting transfers between devices: 17.6 us -> none  [the longest x4 8.84 us: padded_2(): after = lax.ppermute(leading, axis, down)]
    ppermute x10 -> x0, waiting for transfers between devices: 6.12 us -> none  [the longest x4 3.83 us: padded_2(): after = lax.ppermute(leading, axis, down)]
    add x4 -> x0, other arithmetic: 3.02 us -> none  [the longest x2 1.63 us: tendency(): wind_here[0] * along_x + wind_here[1] * along_y + wind_here[2] * along_z]
    select_n x3 -> x0, other arithmetic: 2.81 us -> none  [the longest x2 2.79 us: ramp(): return jnp.where(offset < fringe_width, RATE * sine * sine, 0.0)]
    mul x14 -> x0, other arithmetic: 1.96 us -> none  [the longest x2 0.62 us: diff_x(): return 0.5 * (field[..., 2:, 1:-1, :] - field[..., :-2, 1:-1, :])]
    unnamed x6 -> x1, local copies, waits for them, and re-layouts: 0.01 us -> 1.87 us
    slice x3 -> x0, local copies, waits for them, and re-layouts: 1.6 us -> none  [the longest x1 0.88 us: padded_2(): last = lax.slice_in_dim(shard, length - width, length, axis=dim)]
  transfers between devices with their start and end apart: 10 -> 0, of which waited for: 4 -> 0; matrix products, arithmetic and copies ran while one was open for 21% -> 0% of each run, Pallas kernels for 0% -> 0%
where the time goes in v1:
time: 23.8 us; the launch traced here: 23.6 us
  Pallas kernels  21.7 us (91%)
  local copies, waits for them, and re-layouts  1.87 us (8%)
    pallas_call x1, Pallas kernels, on_device(): pl.pallas_call(functools.partial(kernel, sizes), out_shape=jax.ShapeDtype...  21.7 us
    unnamed x1, local copies, waits for them, and re-layouts  1.87 us

profile of v1, /device:TPU:0, one launch (start us, length us, event | category | flops | bytes accessed | tf_op | source)
XLA Modules:
  0.0 23.6 jit_solution(2446577335093383020)
XLA Ops:
  0.0 21.7 %adjoint_steps.1 = f32[1,4,16,16,128]{4,3,2,1,0:T(8,128)} custom-call(s32[2]{0:T(128)} %fringe.1, f32[1,3,16,16,128]{4,3,2,1,0:T(8,128)} %wind.1, f32[3,16,16,1,128]{4,3,2,1,0:T(1,128)} %bitcast.3, f32[1,4,16,16,128]{4,3,2,1,0:T(8,128)} %adjoint.1, f32[4,16,16,1,128]{4,3,2,1,0:T(1,128)} %bitcast.2, s32[16,16,128]{2,1,0:T(8,128)} %turbines.1), custom_call_target="tpu_custom_call" | custom-call | tf_op jit(solution)/shard_map/adjoint_steps/pallas_call | solution.py:294
  21.8 1.9 %copy.6 = f32[1,4,16,16,128]{4,3,2,1,0:T(8,128)} copy(f32[1,4,16,16,128]{4,3,2,1,0:T(8,128)} %adjoint_steps.1) | data formatting | bytes 1048576

commit v2 on v1

--- a/solution.py
+++ b/solution.py
@@ -14,7 +14,7 @@
 DRAG = 1.0
 RATE = 3.0
 H = 0.5 * DT
-GROUP = 2
+GROUP = 8
 
 
 def shifted_z(field):
@@ -293,7 +293,7 @@
     anywhere = pl.BlockSpec(memory_space=pltpu.HBM)
     return pl.pallas_call(
         functools.partial(kernel, sizes),
-        out_shape=jax.ShapeDtypeStruct(adjoint.shape, f32),
+        out_shape=pltpu.VMEM(adjoint.shape, f32),
         in_specs=[pl.BlockSpec(memory_space=pltpu.SMEM)] + [anywhere] * 5,
         out_specs=pl.BlockSpec(memory_space=pltpu.VMEM),
         scratch_shapes=[

time: 23.8 us -> 20.9 us (0.88)
  Pallas kernels: 21.7 us -> 19.9 us
  local copies, waits for them, and re-layouts: 1.87 us -> 0.8 us
    pallas_call x1, Pallas kernels: 21.7 us -> 19.9 us  [on_device(): pl.pallas_call(functools.partial(kernel, sizes), out_shape=pltpu.VMEM(adj...]
    unnamed x1, local copies, waits for them, and re-layouts: 1.87 us -> 0.8 us
where the time goes in v2:
time: 20.9 us; the launch traced here: 20.7 us
  Pallas kernels  19.9 us (95%)
  local copies, waits for them, and re-layouts  0.8 us (4%)
    pallas_call x1, Pallas kernels, on_device(): pl.pallas_call(functools.partial(kernel, sizes), out_shape=pltpu.VMEM(adj...  19.9 us
    unnamed x1, local copies, waits for them, and re-layouts  0.8 us

profile of v2, /device:TPU:0, one launch (start us, length us, event | category | flops | bytes accessed | tf_op | source)
XLA Modules:
  0.0 20.7 jit_solution(11712184791960773530)
XLA Ops:
  0.0 19.9 %adjoint_steps.1 = f32[1,4,16,16,128]{4,3,2,1,0:T(8,128)S(1)} custom-call(s32[2]{0:T(128)} %fringe.1, f32[1,3,16,16,128]{4,3,2,1,0:T(8,128)} %wind.1, f32[3,16,16,1,128]{4,3,2,1,0:T(1,128)} %bitcast.3, f32[1,4,16,16,128]{4,3,2,1,0:T(8,128)} %adjoint.1, f32[4,16,16,1,128]{4,3,2,1,0:T(1,128)} %bitcast.2, s32[16,16,128]{2,1,0:T(8,128)} %turbines.1), custom_call_target="tpu_custom_call" | custom-call | tf_op jit(solution)/shard_map/adjoint_steps/pallas_call | solution.py:294
  19.9 0.8 %copy.6 = f32[1,4,16,16,128]{4,3,2,1,0:T(8,128)} copy(f32[1,4,16,16,128]{4,3,2,1,0:T(8,128)S(1)} %adjoint_steps.1) | data formatting | bytes 1048576

commit v3 on v2

v3 whole, which is shorter than its diff:
```python
import functools
import math

import jax
import jax.numpy as jnp
from jax import lax
from jax.experimental import pallas as pl
from jax.experimental.pallas import tpu as pltpu
from jax.sharding import PartitionSpec as P

DT = 0.1
SMAG = 0.1
SOUND_SQ = 4.0
DRAG = 1.0
RATE = 3.0
H = 0.5 * DT
GROUP = 7


def shifted_z(field):
    depth = field.shape[-1]
    lane = lax.broadcasted_iota(jnp.int32, field.shape, 1)
    after = jnp.where(lane == depth - 1, 0.0, pltpu.roll(field, depth - 1, 1))
    before = jnp.where(lane == 0, 0.0, pltpu.roll(field, 1, 1))
    return after, before


def shifted_y(field, row_after, row_before):
    rows = field.shape[0]
    row = lax.broadcasted_iota(jnp.int32, field.shape, 0)
    after = jnp.where(row == rows - 1, row_after, pltpu.roll(field, rows - 1, 0))
    before = jnp.where(row == 0, row_before, pltpu.roll(field, 1, 0))
    return after, before


def neighbours(ext, c, x, rows=None, lower=True, upper=True):
    here = ext[c, x + 1]
    nothing = jnp.zeros_like(here)
    after, before = (0.0, 0.0) if rows is None else (rows[1, c, x], rows[0, c, x])
    yp, ym = shifted_y(here, after, before)
    zp, zm = shifted_z(here)
    xp = ext[c, x + 2] if upper else nothing
    xm = ext[c, x] if lower else nothing
    return here, xp, xm, yp, ym, zp, zm


def kernel(
    sizes,
    fringe,
    wind,
    adjoint,
    turbines,
    out,
    a_ext,
    w_ext,
    n_ext,
    b_ext,
    turb,
    coef,
    a_in,
    w_in,
    n_in,
    b_in,
    a_out,
    w_out,
    n_out,
    b_out,
    first_main,
    second_main,
    rates,
    load_sem,
    send_sem,
    recv_sem,
):
    n_gx, n_gy = sizes
    cells_x, cells_y, cells_z = turb.shape
    dom, gx, gy = (lax.axis_index(a) for a in ("dom", "gx", "gy"))
    total = cells_x * n_gx
    reach = total // 4 - 1
    is_main = dom == 0
    in_fringe = jnp.logical_or(gx == n_gx - 1, gx * cells_x < reach)
    sends_forcing = jnp.logical_and(is_main, in_fringe)
    gets_forcing = jnp.logical_and(jnp.logical_not(is_main), in_fringe)
    up_x, down_x = lax.rem(gx + 1, n_gx), lax.rem(gx + n_gx - 1, n_gx)
    up_y, down_y = lax.rem(gy + 1, n_gy), lax.rem(gy + n_gy - 1, n_gy)
    places = ({"gx": up_x}, {"gx": down_x}, {"gy": up_y}, {"gy": down_y})
    partner = {"dom": 1 - dom}

    def remote(src, dst, slot, device):
        return pltpu.make_async_remote_copy(
            src_ref=src,
            dst_ref=dst,
            send_sem=send_sem.at[slot],
            recv_sem=recv_sem.at[slot],
            device_id=device,
            device_id_type=pl.DeviceIdType.MESH,
        )

    load_wind = pltpu.make_async_copy(wind.at[0], w_ext.at[:, pl.ds(1, cells_x)], load_sem.at[0])
    load_adjoint = pltpu.make_async_copy(
        adjoint.at[0], a_ext.at[:, pl.ds(1, cells_x)], load_sem.at[1]
    )
    load_turbines = pltpu.make_async_copy(turbines, turb, load_sem.at[2])
    load_wind.start()

    barrier = pltpu.get_barrier_semaphore()
    for place in places + (partner,):
        pl.semaphore_signal(
            barrier, inc=1, device_id=place, device_id_type=pl.DeviceIdType.MESH
        )
    load_adjoint.start()
    load_turbines.start()

    position = gx * cells_x + lax.broadcasted_iota(jnp.int32, (cells_x, cells_z), 0)
    offset = position - fringe[0]
    offset = jnp.where(offset < 0, offset + total, offset)
    phase = math.pi * (offset.astype(jnp.float32) + 0.5) / fringe[1].astype(jnp.float32)
    sine = jnp.sin(phase)
    sign = jnp.where(is_main, -DT, DT)
    rates[...] = jnp.where(offset < fringe[1], sign * (RATE * sine * sine), 0.0)

    def for_slabs(body):
        body(0, lower=False)
        body(cells_x - 1, upper=False)
        inner = cells_x - 2
        size = max(g for g in range(1, GROUP + 1) if inner % g == 0)

        def several(i, carry):
            for k in range(size):
                body(1 + i * size + k)
            return carry

        lax.fori_loop(0, inner // size, several, 0)

    first_row, last_row = pl.ds(0, 1), pl.ds(cells_y - 1, 1)

    def pack(ext, packed, comps):
        def body(x, **_):
            for c in range(comps):
                packed[0, c, x] = ext[c, x + 1, last_row]
                packed[1, c, x] = ext[c, x + 1, first_row]

        for_slabs(body)

    load_wind.wait()
    pack(w_ext, w_out, 3)
    load_adjoint.wait()
    pack(a_ext, a_out, 4)
    pl.semaphore_wait(barrier, len(places) + 1)

    def exchange(slot, ext, packed, sides):
        pieces = (
            remote(ext.at[:, cells_x], ext.at[:, 0], slot, places[0]),
            remote(ext.at[:, 1], ext.at[:, cells_x + 1], slot + 1, places[1]),
            remote(packed.at[0], sides.at[0], slot + 2, places[2]),
            remote(packed.at[1], sides.at[1], slot + 3, places[3]),
        )
        for k in (2, 3, 0, 1):
            pieces[k].start()
        return pieces

    wind_copies = exchange(0, w_ext, w_out, w_in)
    adjoint_copies = exchange(4, a_ext, a_out, a_in)
    inside = pl.ds(1, cells_x)
    first_forcing = remote(a_ext.at[pl.ds(0, 3), inside], first_main, 16, partner)

    @pl.when(sends_forcing)
    def _():
        first_forcing.start()

    for piece in wind_copies:
        piece.wait_recv()

    def viscosity(x, **_):
        grads = []
        for c in range(3):
            _, xp, xm, yp, ym, zp, zm = neighbours(w_ext, c, x, w_in)
            grads.append((xp - xm, yp - ym, zp - zm))
        own = sum(grads[k][k] * grads[k][k] for k in range(3))
        xy = grads[0][1] + grads[1][0]
        xz = grads[0][2] + grads[2][0]
        yz = grads[1][2] + grads[2][1]
        nu = (0.5 * SMAG) * jnp.sqrt(2.0 * own + (xy * xy + xz * xz + yz * yz))
        n_ext[0, x + 1] = nu
        n_out[0, 0, x] = nu[cells_y - 1 :]
        n_out[1, 0, x] = nu[:1]

    for_slabs(viscosity)
    viscosity_copies = exchange(8, n_ext, n_out, n_in)

    load_turbines.wait()
    for piece in adjoint_copies:
        piece.wait_recv()

    drag_scale = jnp.where(is_main, DT * DRAG, 0.0)
    own_scale = jnp.where(is_main, 1.0, 0.0)

    def coefficients(x, **edges):
        u, v, w = w_ext[0, x + 1], w_ext[1, x + 1], w_ext[2, x + 1]
        nu, *faces = neighbours(n_ext, 0, x, **edges)
        nxp, nxm, nyp, nym, nzp, nzm = (face + nu for face in faces)
        speed = jnp.sqrt(u * u + v * v + w * w)
        drag = drag_scale * turb[x].astype(jnp.float32) * speed
        around = (nxp + nxm) + (nyp + nym) + (nzp + nzm)
        forcing = own_scale * rates[pl.ds(x, 1)]
        return (
            (1.0 + forcing) - H * around - drag,
            H * (nxp + u),
            H * (nxm - u),
            H * (nyp + v),
            H * (nym - v),
            H * (nzp + w),
            H * (nzm - w),
        )

    def advance(ext, weights, x, **edges):
        u, v, w = w_ext[0, x + 1], w_ext[1, x + 1], w_ext[2, x + 1]
        p, pxp, pxm, pyp, pym, pzp, pzm = neighbours(ext, 3, x, **edges)
        slopes = (pxp - pxm, pyp - pym, pzp - pzm)
        gain = u * slopes[0] + v * slopes[1] + w * slopes[2]
        results = []
        for c in range(3):
            stencil = neighbours(ext, c, x, **edges)
            gain = gain + (stencil[1 + 2 * c] - stencil[2 + 2 * c])
            new = sum(k * f for k, f in zip(weights, stencil))
            results.append(new + (SOUND_SQ * H) * slopes[c])
        results.append(p + H * gain)
        return results

    def first_step(x, **edges):
        weights = coefficients(x, **edges)
        for k, weight in enumerate(weights):
            coef[k, x] = weight
        for c, new in enumerate(advance(a_ext, weights, x, rows=a_in)):
            b_ext[c, x + 1] = new
        b_out[0, 3, x] = new[cells_y - 1 :]
        b_out[1, 3, x] = new[:1]

    for_slabs(first_step)

    @pl.when(gets_forcing)
    def _():
        first_forcing.wait_recv()

        def add(x, **_):
            rate = rates[pl.ds(x, 1)]
            for c in range(3):
                b_ext[c, x + 1] += rate * first_main[c, x]

        for_slabs(add)

    for piece in viscosity_copies:
        piece.wait_recv()
    ends = ((0, 0, 2), (cells_x - 1, cells_x + 1, 1))
    edges_y = ((0, first_row, 4), (1, last_row, 3))
    for x, halo, _ in ends:
        nu = H * n_ext[0, halo]
        for c in range(3):
            b_ext[c, x + 1] += nu * (a_ext[c, halo] - a_ext[c, x + 1])

    def first_rows(x, **_):
        for side, row, _ in edges_y:
            nu = H * n_in[side, 0, x]
            for c in range(3):
                change = nu * (a_in[side, c, x] - a_ext[c, x + 1, row])
                new = b_ext[c, x + 1, row] + change
                b_ext[c, x + 1, row] = new
                b_out[1 - side, c, x] = new

    for_slabs(first_rows)
    second_copies = exchange(12, b_ext, b_out, b_in)
    second_forcing = remote(b_ext.at[pl.ds(0, 3), inside], second_main, 17, partner)

    @pl.when(sends_forcing)
    def _():
        second_forcing.start()

    for x, halo, k in ends:
        nu = H * n_ext[0, halo]
        coef[0, x] -= nu
        coef[k, x] += nu

    def coefficient_rows(x, **_):
        for side, row, k in edges_y:
            nu = H * n_in[side, 0, x]
            coef[0, x, row] -= nu
            coef[k, x, row] += nu

    for_slabs(coefficient_rows)

    def second_step(x, **edges):
        weights = tuple(coef[k, x] for k in range(7))
        for c, new in enumerate(advance(b_ext, weights, x, **edges)):
            out[0, c, x] = new

    for_slabs(second_step)

    for piece in second_copies:
        piece.wait_recv()

    def halo_terms(weight, velocity, layer, along, sign):
        terms = [weight * layer[c] for c in range(3)]
        terms[along] = terms[along] + (sign * SOUND_SQ * H) * layer[3]
        terms.append((sign * H) * (velocity * layer[3] + layer[along]))
        return terms

    for x, halo, k in ends:
        layer = [b_ext[c, halo] for c in range(4)]
        sign = -1.0 if k == 2 else 1.0
        for c, term in enumerate(halo_terms(coef[k, x], w_ext[0, x + 1], layer, 0, sign)):
            out[0, c, x] += term

    def second_rows(x, **_):
        for side, row, k in edges_y:
            layer = [b_in[side, c, x] for c in range(4)]
            sign = -1.0 if side == 0 else 1.0
            terms = halo_terms(coef[k, x, row], w_ext[1, x + 1, row], layer, 1, sign)
            for c, term in enumerate(terms):
                out[0, c, x, row] += term

    for_slabs(second_rows)

    @pl.when(gets_forcing)
    def _():
        second_forcing.wait_recv()

        def add(x, **_):
            rate = rates[pl.ds(x, 1)]
            for c in range(3):
                out[0, c, x] += rate * second_main[c, x]

        for_slabs(add)

    for piece in wind_copies + adjoint_copies + viscosity_copies + second_copies:
        piece.wait_send()

    @pl.when(sends_forcing)
    def _():
        first_forcing.wait_send()
        second_forcing.wait_send()


def on_device(wind, adjoint, turbines, fringe_range):
    _, _, cx, cy, cz = wind.shape
    f32 = jnp.float32
    sizes = (lax.axis_size("gx"), lax.axis_size("gy"))
    anywhere = pl.BlockSpec(memory_space=pltpu.HBM)
    return pl.pallas_call(
        functools.partial(kernel, sizes),
        out_shape=pltpu.VMEM(adjoint.shape, f32),
        in_specs=[pl.BlockSpec(memory_space=pltpu.SMEM)] + [anywhere] * 3,
        out_specs=pl.BlockSpec(memory_space=pltpu.VMEM),
        scratch_shapes=[
            pltpu.VMEM((4, cx + 2, cy, cz), f32),
            pltpu.VMEM((3, cx + 2, cy, cz), f32),
            pltpu.VMEM((1, cx + 2, cy, cz), f32),
            pltpu.VMEM((4, cx + 2, cy, cz), f32),
            pltpu.VMEM((cx, cy, cz), jnp.int32),
            pltpu.VMEM((7, cx, cy, cz), f32),
            pltpu.VMEM((2, 4, cx, 1, cz), f32),
            pltpu.VMEM((2, 3, cx, 1, cz), f32),
            pltpu.VMEM((2, 1, cx, 1, cz), f32),
            pltpu.VMEM((2, 4, cx, 1, cz), f32),
            pltpu.VMEM((2, 4, cx, 1, cz), f32),
            pltpu.VMEM((2, 3, cx, 1, cz), f32),
            pltpu.VMEM((2, 1, cx, 1, cz), f32),
            pltpu.VMEM((2, 4, cx, 1, cz), f32),
            pltpu.VMEM((3, cx, cy, cz), f32),
            pltpu.VMEM((3, cx, cy, cz), f32),
            pltpu.VMEM((cx, cz), f32),
            pltpu.SemaphoreType.DMA((3,)),
            pltpu.SemaphoreType.DMA((18,)),
            pltpu.SemaphoreType.DMA((18,)),
        ],
        compiler_params=pltpu.CompilerParams(
            collective_id=0, has_side_effects=True, vmem_limit_bytes=60 * 1024 * 1024
        ),
        name="adjoint_steps",
    )(
        fringe_range,
        wind,
        adjoint,
        turbines,
    )


def solution(mesh):
    in_specs = (
        P("dom", None, "gx", "gy", None),
        P("dom", None, "gx", "gy", None),
        P("gx", "gy", None),
        P(),
    )
    out_specs = P("dom", None, "gx", "gy", None)
    return jax.shard_map(
        on_device, mesh=mesh, in_specs=in_specs, out_specs=out_specs, check_vma=False
    )
```

time: 20.9 us -> 19.8 us (0.947)
  Pallas kernels: 19.9 us -> 18.8 us
    pallas_call x1, Pallas kernels: 19.9 us -> 18.8 us  [on_device(): pl.pallas_call(functools.partial(kernel, sizes), out_shape=pltpu.VMEM(adj...]
where the time goes in v3:
time: 19.8 us; the launch traced here: 19.6 us
  Pallas kernels  18.8 us (95%)
  local copies, waits for them, and re-layouts  0.8 us (4%)
    pallas_call x1, Pallas kernels, on_device(): pl.pallas_call(functools.partial(kernel, sizes), out_shape=pltpu.VMEM(adj...  18.8 us
    unnamed x1, local copies, waits for them, and re-layouts  0.8 us

profile of v3, /device:TPU:0, one launch (start us, length us, event | category | flops | bytes accessed | tf_op | source)
XLA Modules:
  0.0 19.6 jit_solution(18016220133943856359)
XLA Ops:
  0.0 18.8 %adjoint_steps.1 = f32[1,4,16,16,128]{4,3,2,1,0:T(8,128)S(1)} custom-call(s32[2]{0:T(128)} %fringe.1, f32[1,3,16,16,128]{4,3,2,1,0:T(8,128)} %wind.1, f32[1,4,16,16,128]{4,3,2,1,0:T(8,128)} %adjoint.1, s32[16,16,128]{2,1,0:T(8,128)} %turbines.1), custom_call_target="tpu_custom_call" | custom-call | tf_op jit(solution)/shard_map/adjoint_steps/pallas_call | solution.py:348
  18.8 0.8 %copy.6 = f32[1,4,16,16,128]{4,3,2,1,0:T(8,128)} copy(f32[1,4,16,16,128]{4,3,2,1,0:T(8,128)S(1)} %adjoint_steps.1) | data formatting | bytes 1048576

commit v4 on v3

v4 whole, which is shorter than its diff:
```python
import functools
import math

import jax
import jax.numpy as jnp
from jax import lax
from jax.experimental import pallas as pl
from jax.experimental.pallas import tpu as pltpu
from jax.sharding import PartitionSpec as P

DT = 0.1
SMAG = 0.1
SOUND_SQ = 4.0
DRAG = 1.0
RATE = 3.0
H = 0.5 * DT
GROUP = 7


def shifted_z(field):
    depth = field.shape[-1]
    lane = lax.broadcasted_iota(jnp.int32, field.shape, 1)
    after = jnp.where(lane == depth - 1, 0.0, pltpu.roll(field, depth - 1, 1))
    before = jnp.where(lane == 0, 0.0, pltpu.roll(field, 1, 1))
    return after, before


def shifted_y(field):
    rows = field.shape[0]
    row = lax.broadcasted_iota(jnp.int32, field.shape, 0)
    after = jnp.where(row == rows - 1, 0.0, pltpu.roll(field, rows - 1, 0))
    before = jnp.where(row == 0, 0.0, pltpu.roll(field, 1, 0))
    return after, before


def kernel(
    sizes,
    fringe_hbm,
    wind,
    adjoint,
    turbines,
    out,
    a_ext,
    w_ext,
    n_ext,
    b_ext,
    turb,
    coef,
    a_in,
    w_in,
    n_in,
    b_in,
    a_out,
    w_out,
    n_out,
    b_out,
    first_main,
    second_main,
    rates,
    fringe,
    load_sem,
    send_sem,
    recv_sem,
):
    n_gx, n_gy, cells_x, cells_y = sizes
    cells_z = turb.shape[-1]
    dom, gx, gy = (lax.axis_index(a) for a in ("dom", "gx", "gy"))
    total = cells_x * n_gx
    reach = total // 4 - 1
    is_main = dom == 0
    in_fringe = jnp.logical_or(gx == n_gx - 1, gx * cells_x < reach)
    sends_forcing = jnp.logical_and(is_main, in_fringe)
    gets_forcing = jnp.logical_and(jnp.logical_not(is_main), in_fringe)
    up_x, down_x = lax.rem(gx + 1, n_gx), lax.rem(gx + n_gx - 1, n_gx)
    up_y, down_y = lax.rem(gy + 1, n_gy), lax.rem(gy + n_gy - 1, n_gy)
    places = ({"gx": up_x}, {"gx": down_x}, {"gy": up_y}, {"gy": down_y})
    partner = {"dom": 1 - dom}

    def remote(src, dst, slot, device):
        return pltpu.make_async_remote_copy(
            src_ref=src,
            dst_ref=dst,
            send_sem=send_sem.at[slot],
            recv_sem=recv_sem.at[slot],
            device_id=device,
            device_id_type=pl.DeviceIdType.MESH,
        )

    inside = pl.ds(cells_y, cells_x * cells_y)
    load_fringe = pltpu.make_async_copy(fringe_hbm, fringe, load_sem.at[3])
    load_wind = pltpu.make_async_copy(wind, w_ext.at[:, inside], load_sem.at[0])
    load_adjoint = pltpu.make_async_copy(adjoint, a_ext.at[:, inside], load_sem.at[1])
    load_turbines = pltpu.make_async_copy(turbines, turb, load_sem.at[2])

    barrier = pltpu.get_barrier_semaphore()
    for place in places + (partner,):
        pl.semaphore_signal(
            barrier, inc=1, device_id=place, device_id_type=pl.DeviceIdType.MESH
        )
    load_wind.start()
    load_fringe.start()
    load_adjoint.start()
    load_turbines.start()
    pl.semaphore_wait(barrier, len(places) + 1)

    def slab(x):
        return pl.ds(pl.multiple_of(x * cells_y, 8), cells_y)

    def row(y, shift=0):
        return pl.ds(shift * cells_y + y, cells_x, stride=cells_y)

    def copies_x(slot, ext, last, first):
        pieces = (
            remote(last, ext.at[:, slab(0)], slot, places[0]),
            remote(first, ext.at[:, slab(cells_x + 1)], slot + 1, places[1]),
        )
        for piece in pieces:
            piece.start()
        return pieces

    def copies_y(slot, packed, sides):
        pieces = (
            remote(packed.at[0], sides.at[0], slot + 2, places[2]),
            remote(packed.at[1], sides.at[1], slot + 3, places[3]),
        )
        for piece in pieces:
            piece.start()
        return pieces

    def pack(ext, packed, comps):
        for c in range(comps):
            packed[0, c] = ext[c, row(cells_y - 1, 1)]
            packed[1, c] = ext[c, row(0, 1)]

    wind_copies = copies_x(0, w_ext, wind.at[:, slab(cells_x - 1)], wind.at[:, slab(0)])
    adjoint_copies = copies_x(
        4, a_ext, adjoint.at[:, slab(cells_x - 1)], adjoint.at[:, slab(0)]
    )
    load_wind.wait()
    pack(w_ext, w_out, 3)
    wind_copies += copies_y(0, w_out, w_in)
    load_adjoint.wait()
    pack(a_ext, a_out, 4)
    adjoint_copies += copies_y(4, a_out, a_in)
    first_forcing = remote(a_ext.at[pl.ds(0, 3), inside], first_main, 16, partner)

    @pl.when(sends_forcing)
    def _():
        first_forcing.start()

    def for_inner(body):
        inner = cells_x - 2
        size = max(g for g in range(1, GROUP + 1) if inner % g == 0)

        def several(i, carry):
            for k in range(size):
                body(1 + i * size + k)
            return carry

        lax.fori_loop(0, inner // size, several, 0)

    def for_slabs(body):
        body(0, lower=False)
        body(cells_x - 1, upper=False)
        for_inner(body)

    def neighbours(ext, c, x, lower=True, upper=True):
        here = ext[c, slab(x + 1)]
        nothing = jnp.zeros_like(here)
        xp = ext[c, slab(x + 2)] if upper else nothing
        xm = ext[c, slab(x)] if lower else nothing
        return (here, xp, xm, *shifted_y(here), *shifted_z(here))

    def strain(stencils):
        grads = []
        for _, xp, xm, yp, ym, zp, zm in stencils:
            grads.append((xp - xm, yp - ym, zp - zm))
        own = sum(grads[k][k] * grads[k][k] for k in range(3))
        xy = grads[0][1] + grads[1][0]
        xz = grads[0][2] + grads[2][0]
        yz = grads[1][2] + grads[2][1]
        return (0.5 * SMAG) * jnp.sqrt(2.0 * own + (xy * xy + xz * xz + yz * yz))

    def viscosity(x):
        n_ext[0, slab(x + 1)] = strain([neighbours(w_ext, c, x) for c in range(3)])

    for_inner(viscosity)
    for piece in wind_copies:
        piece.wait_recv()
    viscosity(0)
    viscosity(cells_x - 1)
    for side, y, inward in ((0, 0, 1), (1, cells_y - 1, cells_y - 2)):
        stencils = []
        for c in range(3):
            here, halo, near = w_ext[c, row(y, 1)], w_in[side, c], w_ext[c, row(inward, 1)]
            along_y = (near, halo) if side == 0 else (halo, near)
            along_x = (w_ext[c, row(y, 2)], w_ext[c, row(y, 0)])
            stencils.append((here, *along_x, *along_y, *shifted_z(here)))
        nu = strain(stencils)
        n_out[1 - side, 0] = nu
        n_ext[0, row(y, 1)] = nu
    viscosity_copies = copies_y(8, n_out, n_in)
    viscosity_copies += copies_x(8, n_ext, n_ext.at[:, slab(cells_x)], n_ext.at[:, slab(1)])

    load_fringe.wait()
    position = gx * cells_x + lax.broadcasted_iota(jnp.int32, (cells_x, cells_z), 0)
    offset = position - fringe[0]
    offset = jnp.where(offset < 0, offset + total, offset)
    phase = math.pi * (offset.astype(jnp.float32) + 0.5) / fringe[1].astype(jnp.float32)
    sine = jnp.sin(phase)
    sign = jnp.where(is_main, -DT, DT)
    rates[...] = jnp.where(offset < fringe[1], sign * (RATE * sine * sine), 0.0)

    load_turbines.wait()
    drag_scale = jnp.where(is_main, DT * DRAG, 0.0)
    own_scale = jnp.where(is_main, 1.0, 0.0)

    def coefficients(x, **edges):
        u, v, w = (w_ext[c, slab(x + 1)] for c in range(3))
        nu, *faces = neighbours(n_ext, 0, x, **edges)
        nxp, nxm, nyp, nym, nzp, nzm = (face + nu for face in faces)
        speed = jnp.sqrt(u * u + v * v + w * w)
        drag = drag_scale * turb[slab(x)].astype(jnp.float32) * speed
        around = (nxp + nxm) + (nyp + nym) + (nzp + nzm)
        forcing = own_scale * rates[pl.ds(x, 1)]
        return (
            (1.0 + forcing) - H * around - drag,
            H * (nxp + u),
            H * (nxm - u),
            H * (nyp + v),
            H * (nym - v),
            H * (nzp + w),
            H * (nzm - w),
        )

    def advance(ext, weights, x, **edges):
        u, v, w = (w_ext[c, slab(x + 1)] for c in range(3))
        p, pxp, pxm, pyp, pym, pzp, pzm = neighbours(ext, 3, x, **edges)
        slopes = (pxp - pxm, pyp - pym, pzp - pzm)
        gain = u * slopes[0] + v * slopes[1] + w * slopes[2]
        results = []
        for c in range(3):
            stencil = neighbours(ext, c, x, **edges)
            gain = gain + (stencil[1 + 2 * c] - stencil[2 + 2 * c])
            new = sum(k * f for k, f in zip(weights, stencil))
            results.append(new + (SOUND_SQ * H) * slopes[c])
        results.append(p + H * gain)
        return results

    def first_step(x, **edges):
        weights = coefficients(x, **edges)
        for k, weight in enumerate(weights):
            coef[k, slab(x)] = weight
        for c, new in enumerate(advance(a_ext, weights, x, **edges)):
            b_ext[c, slab(x + 1)] = new

    for_slabs(first_step)

    @pl.when(gets_forcing)
    def _():
        first_forcing.wait_recv()

        def add(x, **_):
            rate = rates[pl.ds(x, 1)]
            for c in range(3):
                b_ext[c, slab(x + 1)] += rate * first_main[c, slab(x)]

        for_slabs(add)

    def of_side(side):
        return lambda ext, sides, c: sides[side, c]

    def of_slab(x):
        return lambda ext, sides, c: ext[c, slab(x)]

    layers = (
        (slab(0), slab(1), of_slab(0), 2, 0, -1.0),
        (slab(cells_x - 1), slab(cells_x), of_slab(cells_x + 1), 1, 0, 1.0),
        (row(0), row(0, 1), of_side(0), 4, 1, -1.0),
        (row(cells_y - 1), row(cells_y - 1, 1), of_side(1), 3, 1, 1.0),
    )

    def halo_terms(weight, velocity, layer, along, sign):
        terms = [weight * layer[c] for c in range(3)]
        terms[along] = terms[along] + (sign * SOUND_SQ * H) * layer[3]
        terms.append((sign * H) * (velocity * layer[3] + layer[along]))
        return terms

    for piece in adjoint_copies + viscosity_copies:
        piece.wait_recv()
    for place, extended, layer_of, k, along, sign in layers:
        nu = H * layer_of(n_ext, n_in, 0)
        weight = coef[k, place] + nu
        coef[k, place] = weight
        coef[0, place] -= nu
        layer = [layer_of(a_ext, a_in, c) for c in range(4)]
        terms = halo_terms(weight, w_ext[along, extended], layer, along, sign)
        for c in range(4):
            new = b_ext[c, extended] + terms[c]
            if c < 3:
                new = new - nu * a_ext[c, extended]
            b_ext[c, extended] = new
            if along == 1:
                b_out[1 if sign < 0 else 0, c] = new
    second_copies = copies_y(12, b_out, b_in)
    second_copies += copies_x(12, b_ext, b_ext.at[:, slab(cells_x)], b_ext.at[:, slab(1)])
    second_forcing = remote(b_ext.at[pl.ds(0, 3), inside], second_main, 17, partner)

    @pl.when(sends_forcing)
    def _():
        second_forcing.start()

    def second_step(x, **edges):
        weights = tuple(coef[k, slab(x)] for k in range(7))
        for c, new in enumerate(advance(b_ext, weights, x, **edges)):
            out[c, slab(x)] = new

    for_slabs(second_step)

    for piece in second_copies:
        piece.wait_recv()
    for place, extended, layer_of, k, along, sign in layers:
        layer = [layer_of(b_ext, b_in, c) for c in range(4)]
        terms = halo_terms(coef[k, place], w_ext[along, extended], layer, along, sign)
        for c in range(4):
            out[c, place] += terms[c]

    @pl.when(gets_forcing)
    def _():
        second_forcing.wait_recv()

        def add(x, **_):
            rate = rates[pl.ds(x, 1)]
            for c in range(3):
                out[c, slab(x)] += rate * second_main[c, slab(x)]

        for_slabs(add)

    for piece in wind_copies + adjoint_copies + viscosity_copies + second_copies:
        piece.wait_send()

    @pl.when(sends_forcing)
    def _():
        first_forcing.wait_send()
        second_forcing.wait_send()


def on_device(wind, adjoint, turbines, fringe_range):
    _, _, cx, cy, cz = wind.shape
    f32 = jnp.float32
    sizes = (lax.axis_size("gx"), lax.axis_size("gy"), cx, cy)
    around, tile = (cx + 2) * cy, cx * cy
    later = pl.pallas_call(
        functools.partial(kernel, sizes),
        out_shape=pltpu.VMEM((4, tile, cz), f32),
        in_specs=[pl.BlockSpec(memory_space=pltpu.HBM)] * 4,
        out_specs=pl.BlockSpec(memory_space=pltpu.VMEM),
        scratch_shapes=[
            pltpu.VMEM((4, around, cz), f32),
            pltpu.VMEM((3, around, cz), f32),
            pltpu.VMEM((1, around, cz), f32),
            pltpu.VMEM((4, around, cz), f32),
            pltpu.VMEM((tile, cz), jnp.int32),
            pltpu.VMEM((7, tile, cz), f32),
            pltpu.VMEM((2, 4, cx, cz), f32),
            pltpu.VMEM((2, 3, cx, cz), f32),
            pltpu.VMEM((2, 1, cx, cz), f32),
            pltpu.VMEM((2, 4, cx, cz), f32),
            pltpu.VMEM((2, 4, cx, cz), f32),
            pltpu.VMEM((2, 3, cx, cz), f32),
            pltpu.VMEM((2, 1, cx, cz), f32),
            pltpu.VMEM((2, 4, cx, cz), f32),
            pltpu.VMEM((3, tile, cz), f32),
            pltpu.VMEM((3, tile, cz), f32),
            pltpu.VMEM((cx, cz), f32),
            pltpu.SMEM((2,), jnp.int32),
            pltpu.SemaphoreType.DMA((4,)),
            pltpu.SemaphoreType.DMA((18,)),
            pltpu.SemaphoreType.DMA((18,)),
        ],
        compiler_params=pltpu.CompilerParams(
            collective_id=0, has_side_effects=True, vmem_limit_bytes=60 * 1024 * 1024
        ),
        name="adjoint_steps",
    )(
        fringe_range,
        wind.reshape(3, tile, cz),
        adjoint.reshape(4, tile, cz),
        turbines.reshape(tile, cz),
    )
    return later.reshape(adjoint.shape)


def solution(mesh):
    in_specs = (
        P("dom", None, "gx", "gy", None),
        P("dom", None, "gx", "gy", None),
        P("gx", "gy", None),
        P(),
    )
    out_specs = P("dom", None, "gx", "gy", None)
    return jax.shard_map(
        on_device, mesh=mesh, in_specs=in_specs, out_specs=out_specs, check_vma=False
    )
```

time: 19.8 us -> 18.7 us (0.944)
  Pallas kernels: 18.8 us -> 17.7 us
    pallas_call x1, Pallas kernels: 18.8 us -> 17.7 us  [on_device(): pl.pallas_call(functools.partial(kernel, sizes), out_shape=pltpu.VMEM((4,...]
where the time goes in v4:
time: 18.7 us; the launch traced here: 18.5 us
  Pallas kernels  17.7 us (95%)
  local copies, waits for them, and re-layouts  0.8 us (4%)
    pallas_call x1, Pallas kernels, on_device(): pl.pallas_call(functools.partial(kernel, sizes), out_shape=pltpu.VMEM((4,...  17.7 us
    unnamed x1, local copies, waits for them, and re-layouts  0.8 us

profile of v4, /device:TPU:0, one launch (start us, length us, event | category | flops | bytes accessed | tf_op | source)
XLA Modules:
  0.0 18.5 jit_solution(8018348052355545847)
XLA Ops:
  0.0 17.7 %adjoint_steps.1 = f32[4,256,128]{2,1,0:T(8,128)S(1)} custom-call(s32[2]{0:T(128)} %fringe_hbm.1, f32[3,256,128]{2,1,0:T(8,128)} %bitcast.6, f32[4,256,128]{2,1,0:T(8,128)} %bitcast.5, s32[256,128]{1,0:T(8,128)} %bitcast.7), custom_call_target="tpu_custom_call" | custom-call | tf_op jit(solution)/shard_map/adjoint_steps/pallas_call | solution.py:353
  17.7 0.8 %copy.6 = f32[1,4,16,16,128]{4,3,2,1,0:T(8,128)} copy(f32[1,4,16,16,128]{4,3,2,1,0:T(8,128)S(1)} %bitcast.4) | data formatting | bytes 1048576

commit v5 on v4

--- a/solution.py
+++ b/solution.py
@@ -25,11 +25,11 @@
     return after, before
 
 
-def shifted_y(field):
+def shifted_y(field, row_after=0.0, row_before=0.0):
     rows = field.shape[0]
     row = lax.broadcasted_iota(jnp.int32, field.shape, 0)
-    after = jnp.where(row == rows - 1, 0.0, pltpu.roll(field, rows - 1, 0))
-    before = jnp.where(row == 0, 0.0, pltpu.roll(field, 1, 0))
+    after = jnp.where(row == rows - 1, row_after, pltpu.roll(field, rows - 1, 0))
+    before = jnp.where(row == 0, row_before, pltpu.roll(field, 1, 0))
     return after, before
 
 
@@ -52,8 +52,10 @@
     b_in,
     a_out,
     w_out,
-    n_out,
     b_out,
+    corner_in,
+    corner_out,
+    w_row,
     first_main,
     second_main,
     rates,
@@ -75,6 +77,7 @@
     up_y, down_y = lax.rem(gy + 1, n_gy), lax.rem(gy + n_gy - 1, n_gy)
     places = ({"gx": up_x}, {"gx": down_x}, {"gy": up_y}, {"gy": down_y})
     partner = {"dom": 1 - dom}
+    diagonal = tuple({"gx": x, "gy": y} for x in (up_x, down_x) for y in (up_y, down_y))
 
     def remote(src, dst, slot, device):
         return pltpu.make_async_remote_copy(
@@ -87,13 +90,14 @@
         )
 
     inside = pl.ds(cells_y, cells_x * cells_y)
+    inside_wind = pl.ds(2 * cells_y, cells_x * cells_y)
     load_fringe = pltpu.make_async_copy(fringe_hbm, fringe, load_sem.at[3])
-    load_wind = pltpu.make_async_copy(wind, w_ext.at[:, inside], load_sem.at[0])
+    load_wind = pltpu.make_async_copy(wind, w_ext.at[:, inside_wind], load_sem.at[0])
     load_adjoint = pltpu.make_async_copy(adjoint, a_ext.at[:, inside], load_sem.at[1])
     load_turbines = pltpu.make_async_copy(turbines, turb, load_sem.at[2])
 
     barrier = pltpu.get_barrier_semaphore()
-    for place in places + (partner,):
+    for place in places + diagonal + (partner,):
         pl.semaphore_signal(
             barrier, inc=1, device_id=place, device_id_type=pl.DeviceIdType.MESH
         )
@@ -101,7 +105,7 @@
     load_fringe.start()
     load_adjoint.start()
     load_turbines.start()
-    pl.semaphore_wait(barrier, len(places) + 1)
+    pl.semaphore_wait(barrier, len(places) + len(diagonal) + 1)
 
     def slab(x):
         return pl.ds(pl.multiple_of(x * cells_y, 8), cells_y)
@@ -109,10 +113,11 @@
     def row(y, shift=0):
         return pl.ds(shift * cells_y + y, cells_x, stride=cells_y)
 
-    def copies_x(slot, ext, last, first):
+    def copies_x(slot, ext, last, first, depth):
+        span = depth * cells_y
         pieces = (
-            remote(last, ext.at[:, slab(0)], slot, places[0]),
-            remote(first, ext.at[:, slab(cells_x + 1)], slot + 1, places[1]),
+            remote(last, ext.at[:, pl.ds(0, span)], slot, places[0]),
+            remote(first, ext.at[:, pl.ds(cells_x * cells_y + span, span)], slot + 1, places[1]),
         )
         for piece in pieces:
             piece.start()
@@ -127,20 +132,35 @@
             piece.start()
         return pieces
 
-    def pack(ext, packed, comps):
-        for c in range(comps):
-            packed[0, c] = ext[c, row(cells_y - 1, 1)]
-            packed[1, c] = ext[c, row(0, 1)]
-
-    wind_copies = copies_x(0, w_ext, wind.at[:, slab(cells_x - 1)], wind.at[:, slab(0)])
+    span = 2 * cells_y
+    wind_copies = copies_x(
+        0,
+        w_ext,
+        wind.at[:, pl.ds((cells_x - 2) * cells_y, span)],
+        wind.at[:, pl.ds(0, span)],
+        2,
+    )
     adjoint_copies = copies_x(
-        4, a_ext, adjoint.at[:, slab(cells_x - 1)], adjoint.at[:, slab(0)]
+        4, a_ext, adjoint.at[:, slab(cells_x - 1)], adjoint.at[:, slab(0)], 1
     )
     load_wind.wait()
-    pack(w_ext, w_out, 3)
+    for c in range(3):
+        for j in range(2):
+            w_out[0, c, j] = w_ext[c, row(cells_y - 1 - j, 2)]
+            w_out[1, c, j] = w_ext[c, row(j, 2)]
     wind_copies += copies_y(0, w_out, w_in)
+    corner_copies = []
+    for q in range(4):
+        x, y = (cells_x - 1, 0)[q // 2], (cells_y - 1, 0)[q % 2]
+        for c in range(3):
+            corner_out[q, c] = w_ext[c, pl.ds((x + 2) * cells_y + y, 1)]
+        piece = remote(corner_out.at[q], corner_in.at[q], 8 + q, diagonal[q])
+        piece.start()
+        corner_copies.append(piece)
     load_adjoint.wait()
-    pack(a_ext, a_out, 4)
+    for c in range(4):
+        a_out[0, c] = a_ext[c, row(cells_y - 1, 1)]
+        a_out[1, c] = a_ext[c, row(0, 1)]
     adjoint_copies += copies_y(4, a_out, a_in)
     first_forcing = remote(a_ext.at[pl.ds(0, 3), inside], first_main, 16, partner)
 
@@ -164,12 +184,12 @@
         body(cells_x - 1, upper=False)
         for_inner(body)
 
-    def neighbours(ext, c, x, lower=True, upper=True):
-        here = ext[c, slab(x + 1)]
+    def neighbours(ext, c, x, lower=True, upper=True, base=1, rows=(0.0, 0.0)):
+        here = ext[c, slab(x + base)]
         nothing = jnp.zeros_like(here)
-        xp = ext[c, slab(x + 2)] if upper else nothing
-        xm = ext[c, slab(x)] if lower else nothing
-        return (here, xp, xm, *shifted_y(here), *shifted_z(here))
+        xp = ext[c, slab(x + base + 1)] if upper else nothing
+        xm = ext[c, slab(x + base - 1)] if lower else nothing
+        return (here, xp, xm, *shifted_y(here, *rows), *shifted_z(here))
 
     def strain(stencils):
         grads = []
@@ -182,7 +202,7 @@
         return (0.5 * SMAG) * jnp.sqrt(2.0 * own + (xy * xy + xz * xz + yz * yz))
 
     def viscosity(x):
-        n_ext[0, slab(x + 1)] = strain([neighbours(w_ext, c, x) for c in range(3)])
+        n_ext[0, slab(x + 1)] = strain([neighbours(w_ext, c, x, base=2) for c in range(3)])
 
     for_inner(viscosity)
     for piece in wind_copies:
@@ -192,15 +212,11 @@
     for side, y, inward in ((0, 0, 1), (1, cells_y - 1, cells_y - 2)):
         stencils = []
         for c in range(3):
-            here, halo, near = w_ext[c, row(y, 1)], w_in[side, c], w_ext[c, row(inward, 1)]
+            here, halo, near = w_ext[c, row(y, 2)], w_in[side, c, 0], w_ext[c, row(inward, 2)]
             along_y = (near, halo) if side == 0 else (halo, near)
-            along_x = (w_ext[c, row(y, 2)], w_ext[c, row(y, 0)])
+            along_x = (w_ext[c, row(y, 3)], w_ext[c, row(y, 1)])
             stencils.append((here, *along_x, *along_y, *shifted_z(here)))
-        nu = strain(stencils)
-        n_out[1 - side, 0] = nu
-        n_ext[0, row(y, 1)] = nu
-    viscosity_copies = copies_y(8, n_out, n_in)
-    viscosity_copies += copies_x(8, n_ext, n_ext.at[:, slab(cells_x)], n_ext.at[:, slab(1)])
+        n_ext[0, row(y, 1)] = strain(stencils)
 
     load_fringe.wait()
     position = gx * cells_x + lax.broadcasted_iota(jnp.int32, (cells_x, cells_z), 0)
@@ -216,7 +232,7 @@
     own_scale = jnp.where(is_main, 1.0, 0.0)
 
     def coefficients(x, **edges):
-        u, v, w = (w_ext[c, slab(x + 1)] for c in range(3))
+        u, v, w = (w_ext[c, slab(x + 2)] for c in range(3))
         nu, *faces = neighbours(n_ext, 0, x, **edges)
         nxp, nxm, nyp, nym, nzp, nzm = (face + nu for face in faces)
         speed = jnp.sqrt(u * u + v * v + w * w)
@@ -234,7 +250,7 @@
         )
 
     def advance(ext, weights, x, **edges):
-        u, v, w = (w_ext[c, slab(x + 1)] for c in range(3))
+        u, v, w = (w_ext[c, slab(x + 2)] for c in range(3))
         p, pxp, pxm, pyp, pym, pzp, pzm = neighbours(ext, 3, x, **edges)
         slopes = (pxp - pxm, pyp - pym, pzp - pzm)
         gain = u * slopes[0] + v * slopes[1] + w * slopes[2]
@@ -274,10 +290,10 @@
         return lambda ext, sides, c: ext[c, slab(x)]
 
     layers = (
-        (slab(0), slab(1), of_slab(0), 2, 0, -1.0),
-        (slab(cells_x - 1), slab(cells_x), of_slab(cells_x + 1), 1, 0, 1.0),
-        (row(0), row(0, 1), of_side(0), 4, 1, -1.0),
-        (row(cells_y - 1), row(cells_y - 1, 1), of_side(1), 3, 1, 1.0),
+        (slab(0), slab(1), slab(2), of_slab(0), 2, 0, -1.0),
+        (slab(cells_x - 1), slab(cells_x), slab(cells_x + 1), of_slab(cells_x + 1), 1, 0, 1.0),
+        (row(0), row(0, 1), row(0, 2), of_side(0), 4, 1, -1.0),
+        (row(cells_y - 1), row(cells_y - 1, 1), row(cells_y - 1, 2), of_side(1), 3, 1, 1.0),
     )
 
     def halo_terms(weight, velocity, layer, along, sign):
@@ -286,15 +302,36 @@
         terms.append((sign * H) * (velocity * layer[3] + layer[along]))
         return terms
 
-    for piece in adjoint_copies + viscosity_copies:
+    for piece in corner_copies:
         piece.wait_recv()
-    for place, extended, layer_of, k, along, sign in layers:
+    for x, q in ((-1, 0), (cells_x, 2)):
+        n_ext[0, slab(x + 1)] = strain(
+            [
+                neighbours(w_ext, c, x, base=2, rows=(corner_in[q + 1, c], corner_in[q, c]))
+                for c in range(3)
+            ]
+        )
+    for side, y in ((0, 0), (1, cells_y - 1)):
+        stencils = []
+        for c in range(3):
+            here, far, near = w_in[side, c, 0], w_in[side, c, 1], w_ext[c, row(y, 2)]
+            w_row[side, c, pl.ds(8, cells_x)] = here
+            w_row[side, c, pl.ds(7, 1)] = corner_in[side, c]
+            w_row[side, c, pl.ds(8 + cells_x, 1)] = corner_in[2 + side, c]
+            along_x = (w_row[side, c, pl.ds(9, cells_x)], w_row[side, c, pl.ds(7, cells_x)])
+            along_y = (near, far) if side == 0 else (far, near)
+            stencils.append((here, *along_x, *along_y, *shifted_z(here)))
+        n_in[side, 0] = strain(stencils)
+
+    for piece in adjoint_copies:
+        piece.wait_recv()
+    for place, extended, windy, layer_of, k, along, sign in layers:
         nu = H * layer_of(n_ext, n_in, 0)
         weight = coef[k, place] + nu
         coef[k, place] = weight
         coef[0, place] -= nu
         layer = [layer_of(a_ext, a_in, c) for c in range(4)]
-        terms = halo_terms(weight, w_ext[along, extended], layer, along, sign)
+        terms = halo_terms(weight, w_ext[along, windy], layer, along, sign)
         for c in range(4):
             new = b_ext[c, extended] + terms[c]
             if c < 3:
@@ -303,7 +340,7 @@
             if along == 1:
                 b_out[1 if sign < 0 else 0, c] = new
     second_copies = copies_y(12, b_out, b_in)
-    second_copies += copies_x(12, b_ext, b_ext.at[:, slab(cells_x)], b_ext.at[:, slab(1)])
+    second_copies += copies_x(12, b_ext, b_ext.at[:, slab(cells_x)], b_ext.at[:, slab(1)], 1)
     second_forcing = remote(b_ext.at[pl.ds(0, 3), inside], second_main, 17, partner)
 
     @pl.when(sends_forcing)
@@ -319,9 +356,9 @@
 
     for piece in second_copies:
         piece.wait_recv()
-    for place, extended, layer_of, k, along, sign in layers:
+    for place, extended, windy, layer_of, k, along, sign in layers:
         layer = [layer_of(b_ext, b_in, c) for c in range(4)]
-        terms = halo_terms(coef[k, place], w_ext[along, extended], layer, along, sign)
+        terms = halo_terms(coef[k, place], w_ext[along, windy], layer, along, sign)
         for c in range(4):
             out[c, place] += terms[c]
 
@@ -336,7 +373,7 @@
 
         for_slabs(add)
 
-    for piece in wind_copies + adjoint_copies + viscosity_copies + second_copies:
+    for piece in (*wind_copies, *corner_copies, *adjoint_copies, *second_copies):
         piece.wait_send()
 
     @pl.when(sends_forcing)
@@ -349,7 +386,7 @@
     _, _, cx, cy, cz = wind.shape
     f32 = jnp.float32
     sizes = (lax.axis_size("gx"), lax.axis_size("gy"), cx, cy)
-    around, tile = (cx + 2) * cy, cx * cy
+    around, tile, wide = (cx + 2) * cy, cx * cy, (cx + 4) * cy
     later = pl.pallas_call(
         functools.partial(kernel, sizes),
         out_shape=pltpu.VMEM((4, tile, cz), f32),
@@ -357,19 +394,21 @@
         out_specs=pl.BlockSpec(memory_space=pltpu.VMEM),
         scratch_shapes=[
             pltpu.VMEM((4, around, cz), f32),
-            pltpu.VMEM((3, around, cz), f32),
+            pltpu.VMEM((3, wide, cz), f32),
             pltpu.VMEM((1, around, cz), f32),
             pltpu.VMEM((4, around, cz), f32),
             pltpu.VMEM((tile, cz), jnp.int32),
             pltpu.VMEM((7, tile, cz), f32),
             pltpu.VMEM((2, 4, cx, cz), f32),
-            pltpu.VMEM((2, 3, cx, cz), f32),
+            pltpu.VMEM((2, 3, 2, cx, cz), f32),
             pltpu.VMEM((2, 1, cx, cz), f32),
             pltpu.VMEM((2, 4, cx, cz), f32),
             pltpu.VMEM((2, 4, cx, cz), f32),
-            pltpu.VMEM((2, 3, cx, cz), f32),
-            pltpu.VMEM((2, 1, cx, cz), f32),
+            pltpu.VMEM((2, 3, 2, cx, cz), f32),
             pltpu.VMEM((2, 4, cx, cz), f32),
+            pltpu.VMEM((4, 3, 1, cz), f32),
+            pltpu.VMEM((4, 3, 1, cz), f32),
+            pltpu.VMEM((2, 3, cx + 16, cz), f32),
             pltpu.VMEM((3, tile, cz), f32),
             pltpu.VMEM((3, tile, cz), f32),
             pltpu.VMEM((cx, cz), f32),

time: 18.7 us -> 18.6 us (level)
  no operation moved by 1% of the time
where the time goes in v5:
time: 18.6 us; the launch traced here: 18.4 us
  Pallas kernels  17.6 us (95%)
  local copies, waits for them, and re-layouts  0.8 us (4%)
    pallas_call x1, Pallas kernels, on_device(): pl.pallas_call(functools.partial(kernel, sizes), out_shape=pltpu.VMEM((4,...  17.6 us
    unnamed x1, local copies, waits for them, and re-layouts  0.8 us

profile of v5, /device:TPU:0, one launch (start us, length us, event | category | flops | bytes accessed | tf_op | source)
XLA Modules:
  0.0 18.4 jit_solution(8278998829830953046)
XLA Ops:
  0.0 17.6 %adjoint_steps.1 = f32[4,256,128]{2,1,0:T(8,128)S(1)} custom-call(s32[2]{0:T(128)} %fringe_hbm.1, f32[3,256,128]{2,1,0:T(8,128)} %bitcast.6, f32[4,256,128]{2,1,0:T(8,128)} %bitcast.5, s32[256,128]{1,0:T(8,128)} %bitcast.7), custom_call_target="tpu_custom_call" | custom-call | tf_op jit(solution)/shard_map/adjoint_steps/pallas_call | solution.py:390
  17.6 0.8 %copy.6 = f32[1,4,16,16,128]{4,3,2,1,0:T(8,128)} copy(f32[1,4,16,16,128]{4,3,2,1,0:T(8,128)S(1)} %bitcast.4) | data formatting | bytes 1048576

commit v6 on v5

--- a/solution.py
+++ b/solution.py
@@ -58,6 +58,9 @@
     w_row,
     first_main,
     second_main,
+    staged,
+    main_rows,
+    main_ends,
     rates,
     fringe,
     load_sem,
@@ -269,8 +272,15 @@
             coef[k, slab(x)] = weight
         for c, new in enumerate(advance(a_ext, weights, x, **edges)):
             b_ext[c, slab(x + 1)] = new
+            if c < 3:
+                staged[c, slab(x)] = new
 
     for_slabs(first_step)
+    early_forcing = remote(staged, second_main, 17, partner)
+
+    @pl.when(sends_forcing)
+    def _():
+        early_forcing.start()
 
     @pl.when(gets_forcing)
     def _():
@@ -341,11 +351,17 @@
                 b_out[1 if sign < 0 else 0, c] = new
     second_copies = copies_y(12, b_out, b_in)
     second_copies += copies_x(12, b_ext, b_ext.at[:, slab(cells_x)], b_ext.at[:, slab(1)], 1)
-    second_forcing = remote(b_ext.at[pl.ds(0, 3), inside], second_main, 17, partner)
+    velocities = pl.ds(0, 3)
+    late_forcing = (
+        remote(b_out.at[:, velocities], main_rows, 18, partner),
+        remote(b_ext.at[velocities, slab(1)], main_ends.at[0], 19, partner),
+        remote(b_ext.at[velocities, slab(cells_x)], main_ends.at[1], 20, partner),
+    )
 
     @pl.when(sends_forcing)
     def _():
-        second_forcing.start()
+        for piece in late_forcing:
+            piece.start()
 
     def second_step(x, **edges):
         weights = tuple(coef[k, slab(x)] for k in range(7))
@@ -353,6 +369,17 @@
             out[c, slab(x)] = new
 
     for_slabs(second_step)
+
+    @pl.when(gets_forcing)
+    def _():
+        early_forcing.wait_recv()
+
+        def add(x, **_):
+            rate = rates[pl.ds(x, 1)]
+            for c in range(3):
+                out[c, slab(x)] += rate * second_main[c, slab(x)]
+
+        for_slabs(add)
 
     for piece in second_copies:
         piece.wait_recv()
@@ -364,14 +391,17 @@
 
     @pl.when(gets_forcing)
     def _():
-        second_forcing.wait_recv()
-
-        def add(x, **_):
+        for piece in late_forcing:
+            piece.wait_recv()
+        for end, x in ((0, 0), (1, cells_x - 1)):
             rate = rates[pl.ds(x, 1)]
             for c in range(3):
-                out[c, slab(x)] += rate * second_main[c, slab(x)]
-
-        for_slabs(add)
+                final = main_ends[end, c]
+                out[c, slab(x)] += rate * (final - second_main[c, slab(x)])
+                second_main[c, slab(x)] = final
+        for side, y in ((0, cells_y - 1), (1, 0)):
+            for c in range(3):
+                out[c, row(y)] += rates[...] * (main_rows[side, c] - second_main[c, row(y)])
 
     for piece in (*wind_copies, *corner_copies, *adjoint_copies, *second_copies):
         piece.wait_send()
@@ -379,7 +409,9 @@
     @pl.when(sends_forcing)
     def _():
         first_forcing.wait_send()
-        second_forcing.wait_send()
+        early_forcing.wait_send()
+        for piece in late_forcing:
+            piece.wait_send()
 
 
 def on_device(wind, adjoint, turbines, fringe_range):
@@ -411,11 +443,14 @@
             pltpu.VMEM((2, 3, cx + 16, cz), f32),
             pltpu.VMEM((3, tile, cz), f32),
             pltpu.VMEM((3, tile, cz), f32),
+            pltpu.VMEM((3, tile, cz), f32),
+            pltpu.VMEM((2, 3, cx, cz), f32),
+            pltpu.VMEM((2, 3, cy, cz), f32),
             pltpu.VMEM((cx, cz), f32),
             pltpu.SMEM((2,), jnp.int32),
             pltpu.SemaphoreType.DMA((4,)),
-            pltpu.SemaphoreType.DMA((18,)),
-            pltpu.SemaphoreType.DMA((18,)),
+            pltpu.SemaphoreType.DMA((21,)),
+            pltpu.SemaphoreType.DMA((21,)),
         ],
         compiler_params=pltpu.CompilerParams(
             collective_id=0, has_side_effects=True, vmem_limit_bytes=60 * 1024 * 1024

time: 18.6 us -> 18.6 us (level)
  no operation moved by 1% of the time
where the time goes in v6:
time: 18.6 us; the launch traced here: 18.5 us
  Pallas kernels  17.7 us (95%)
  local copies, waits for them, and re-layouts  0.8 us (4%)
    pallas_call x1, Pallas kernels, on_device(): pl.pallas_call(functools.partial(kernel, sizes), out_shape=pltpu.VMEM((4,...  17.7 us
    unnamed x1, local copies, waits for them, and re-layouts  0.8 us

profile of v6, /device:TPU:0, one launch (start us, length us, event | category | flops | bytes accessed | tf_op | source)
XLA Modules:
  0.0 18.5 jit_solution(15268616468464476161)
XLA Ops:
  0.0 17.7 %adjoint_steps.1 = f32[4,256,128]{2,1,0:T(8,128)S(1)} custom-call(s32[2]{0:T(128)} %fringe_hbm.1, f32[3,256,128]{2,1,0:T(8,128)} %bitcast.6, f32[4,256,128]{2,1,0:T(8,128)} %bitcast.5, s32[256,128]{1,0:T(8,128)} %bitcast.7), custom_call_target="tpu_custom_call" | custom-call | tf_op jit(solution)/shard_map/adjoint_steps/pallas_call | solution.py:422
  17.7 0.8 %copy.6 = f32[1,4,16,16,128]{4,3,2,1,0:T(8,128)} copy(f32[1,4,16,16,128]{4,3,2,1,0:T(8,128)S(1)} %bitcast.4) | data formatting | bytes 1048576

commit v7 on v5

--- a/solution.py
+++ b/solution.py
@@ -14,7 +14,7 @@
 DRAG = 1.0
 RATE = 3.0
 H = 0.5 * DT
-GROUP = 7
+GROUP = 14
 
 
 def shifted_z(field):
@@ -96,14 +96,14 @@
     load_adjoint = pltpu.make_async_copy(adjoint, a_ext.at[:, inside], load_sem.at[1])
     load_turbines = pltpu.make_async_copy(turbines, turb, load_sem.at[2])
 
+    load_wind.start()
+    load_adjoint.start()
     barrier = pltpu.get_barrier_semaphore()
     for place in places + diagonal + (partner,):
         pl.semaphore_signal(
             barrier, inc=1, device_id=place, device_id_type=pl.DeviceIdType.MESH
         )
-    load_wind.start()
     load_fringe.start()
-    load_adjoint.start()
     load_turbines.start()
     pl.semaphore_wait(barrier, len(places) + len(diagonal) + 1)
 

time: 18.6 us -> 18.5 us (level)
  no operation moved by 1% of the time
where the time goes in v7:
time: 18.5 us; the launch traced here: 18.4 us
  Pallas kernels  17.6 us (95%)
  local copies, waits for them, and re-layouts  0.8 us (4%)
    pallas_call x1, Pallas kernels, on_device(): pl.pallas_call(functools.partial(kernel, sizes), out_shape=pltpu.VMEM((4,...  17.6 us
    unnamed x1, local copies, waits for them, and re-layouts  0.8 us

profile of v7, /device:TPU:0, one launch (start us, length us, event | category | flops | bytes accessed | tf_op | source)
XLA Modules:
  0.0 18.4 jit_solution(14210344661973647232)
XLA Ops:
  0.0 17.6 %adjoint_steps.1 = f32[4,256,128]{2,1,0:T(8,128)S(1)} custom-call(s32[2]{0:T(128)} %fringe_hbm.1, f32[3,256,128]{2,1,0:T(8,128)} %bitcast.6, f32[4,256,128]{2,1,0:T(8,128)} %bitcast.5, s32[256,128]{1,0:T(8,128)} %bitcast.7), custom_call_target="tpu_custom_call" | custom-call | tf_op jit(solution)/shard_map/adjoint_steps/pallas_call | solution.py:390
  17.6 0.8 %copy.6 = f32[1,4,16,16,128]{4,3,2,1,0:T(8,128)} copy(f32[1,4,16,16,128]{4,3,2,1,0:T(8,128)S(1)} %bitcast.4) | data formatting | bytes 1048576

commit v8 on v7

--- a/solution.py
+++ b/solution.py
@@ -140,15 +140,20 @@
         wind.at[:, pl.ds(0, span)],
         2,
     )
-    adjoint_copies = copies_x(
-        4, a_ext, adjoint.at[:, slab(cells_x - 1)], adjoint.at[:, slab(0)], 1
-    )
     load_wind.wait()
     for c in range(3):
         for j in range(2):
             w_out[0, c, j] = w_ext[c, row(cells_y - 1 - j, 2)]
             w_out[1, c, j] = w_ext[c, row(j, 2)]
     wind_copies += copies_y(0, w_out, w_in)
+    adjoint_copies = copies_x(
+        4, a_ext, adjoint.at[:, slab(cells_x - 1)], adjoint.at[:, slab(0)], 1
+    )
+    load_adjoint.wait()
+    for c in range(4):
+        a_out[0, c] = a_ext[c, row(cells_y - 1, 1)]
+        a_out[1, c] = a_ext[c, row(0, 1)]
+    adjoint_copies += copies_y(4, a_out, a_in)
     corner_copies = []
     for q in range(4):
         x, y = (cells_x - 1, 0)[q // 2], (cells_y - 1, 0)[q % 2]
@@ -157,11 +162,6 @@
         piece = remote(corner_out.at[q], corner_in.at[q], 8 + q, diagonal[q])
         piece.start()
         corner_copies.append(piece)
-    load_adjoint.wait()
-    for c in range(4):
-        a_out[0, c] = a_ext[c, row(cells_y - 1, 1)]
-        a_out[1, c] = a_ext[c, row(0, 1)]
-    adjoint_copies += copies_y(4, a_out, a_in)
     first_forcing = remote(a_ext.at[pl.ds(0, 3), inside], first_main, 16, partner)
 
     @pl.when(sends_forcing)

time: 18.5 us -> 18.5 us (level)
  no operation moved by 1% of the time
where the time goes in v8:
time: 18.5 us; the launch traced here: 18.4 us
  Pallas kernels  17.5 us (95%)
  local copies, waits for them, and re-layouts  0.8 us (4%)
    pallas_call x1, Pallas kernels, on_device(): pl.pallas_call(functools.partial(kernel, sizes), out_shape=pltpu.VMEM((4,...  17.5 us
    unnamed x1, local copies, waits for them, and re-layouts  0.8 us

profile of v8, /device:TPU:0, one launch (start us, length us, event | category | flops | bytes accessed | tf_op | source)
XLA Modules:
  0.0 18.4 jit_solution(15252784997739673354)
XLA Ops:
  0.0 17.5 %adjoint_steps.1 = f32[4,256,128]{2,1,0:T(8,128)S(1)} custom-call(s32[2]{0:T(128)} %fringe_hbm.1, f32[3,256,128]{2,1,0:T(8,128)} %bitcast.6, f32[4,256,128]{2,1,0:T(8,128)} %bitcast.5, s32[256,128]{1,0:T(8,128)} %bitcast.7), custom_call_target="tpu_custom_call" | custom-call | tf_op jit(solution)/shard_map/adjoint_steps/pallas_call | solution.py:390
  17.6 0.8 %copy.6 = f32[1,4,16,16,128]{4,3,2,1,0:T(8,128)} copy(f32[1,4,16,16,128]{4,3,2,1,0:T(8,128)S(1)} %bitcast.4) | data formatting | bytes 1048576

commit v9 on v5

--- a/solution.py
+++ b/solution.py
@@ -149,6 +149,11 @@
             w_out[0, c, j] = w_ext[c, row(cells_y - 1 - j, 2)]
             w_out[1, c, j] = w_ext[c, row(j, 2)]
     wind_copies += copies_y(0, w_out, w_in)
+    load_adjoint.wait()
+    for c in range(4):
+        a_out[0, c] = a_ext[c, row(cells_y - 1, 1)]
+        a_out[1, c] = a_ext[c, row(0, 1)]
+    adjoint_copies += copies_y(4, a_out, a_in)
     corner_copies = []
     for q in range(4):
         x, y = (cells_x - 1, 0)[q // 2], (cells_y - 1, 0)[q % 2]
@@ -157,11 +162,6 @@
         piece = remote(corner_out.at[q], corner_in.at[q], 8 + q, diagonal[q])
         piece.start()
         corner_copies.append(piece)
-    load_adjoint.wait()
-    for c in range(4):
-        a_out[0, c] = a_ext[c, row(cells_y - 1, 1)]
-        a_out[1, c] = a_ext[c, row(0, 1)]
-    adjoint_copies += copies_y(4, a_out, a_in)
     first_forcing = remote(a_ext.at[pl.ds(0, 3), inside], first_main, 16, partner)
 
     @pl.when(sends_forcing)

time: 18.6 us -> 18.5 us (level)
  no operation moved by 1% of the time
where the time goes in v9:
time: 18.5 us; the launch traced here: 18.4 us
  Pallas kernels  17.6 us (95%)
  local copies, waits for them, and re-layouts  0.8 us (4%)
    pallas_call x1, Pallas kernels, on_device(): pl.pallas_call(functools.partial(kernel, sizes), out_shape=pltpu.VMEM((4,...  17.6 us
    unnamed x1, local copies, waits for them, and re-layouts  0.8 us

profile of v9, /device:TPU:0, one launch (start us, length us, event | category | flops | bytes accessed | tf_op | source)
XLA Modules:
  0.0 18.4 jit_solution(12302103833325790391)
XLA Ops:
  0.0 17.6 %adjoint_steps.1 = f32[4,256,128]{2,1,0:T(8,128)S(1)} custom-call(s32[2]{0:T(128)} %fringe_hbm.1, f32[3,256,128]{2,1,0:T(8,128)} %bitcast.6, f32[4,256,128]{2,1,0:T(8,128)} %bitcast.5, s32[256,128]{1,0:T(8,128)} %bitcast.7), custom_call_target="tpu_custom_call" | custom-call | tf_op jit(solution)/shard_map/adjoint_steps/pallas_call | solution.py:390
  17.6 0.8 %copy.6 = f32[1,4,16,16,128]{4,3,2,1,0:T(8,128)} copy(f32[1,4,16,16,128]{4,3,2,1,0:T(8,128)S(1)} %bitcast.4) | data formatting | bytes 1048576
